TPU v7x, 128 devices: a whole 4x4x4 slice. The times are simulated.
128 devices in a mesh: head: 4 (over x_lo, core), ctx: 32 (over y, x_hi, z).
Axes of the slice: x: 4 (x_hi: 2, x_lo: 2; x = x_hi * 2 + x_lo), y: 4, z: 4, core: 2. Of those that a mesh axis runs over, the one named last changes fastest.
Arguments:
- keys: float32 [2, 6144, 4096], P(None, 'ctx', 'head'), may hold values from -6 to 6
- values: float32 [2, 6144, 4096], P(None, 'ctx', 'head'), may hold values from -6 to 6
- queries: float32 [2, 6144, 4096], P(None, 'ctx', 'head'), may hold values from -6 to 6
- rates: float32 [2, 6144], P(None, 'ctx'), may hold values from 0.05 to 1
- w_first: float32 [8, 512, 512], P('head'), may hold values from -0.25 to 0.25
- w_second: float32 [8, 512, 512], P('head'), may hold values from -0.25 to 0.25
- w_third: float32 [8, 512, 512], P('head'), may hold values from -0.25 to 0.25
- step_size: float32 [8], P('head'), may hold values from 0.2 to 1
- owner_order: int32 [32, 384], P('ctx'), may hold values from 0 to 383, each once within a row
- gate: float32 [32, 384, 4096], P('ctx', 'head'), may hold values from -6 to 6
- gain: float32 [4096], replicated, may hold values from 0.5 to 1.5
Outputs:
- mixed: float32 [32, 384, 4096], P('ctx', 'head')
Inputs may be any that keep to these rules, and one draw needn't show every extreme that they name: Each row of owner_order is a permutation of the 384 tokens of its block.
All inputs are finite; a program needn't handle non-finite values.
Results may differ from a plain program's by a relative error of at most 0.0003.
Values sent between devices are 32-bit elements; how exact they have to be, the bound alone decides.
No kernel may reach another device: no remote copies, remote signals or barrier semaphores. Data moves between devices by JAX's collectives and lax.ppermute only.
A program may use at most 192 MiB of HBM per device.

v0:
```python
import jax
import jax.numpy as jnp
from jax import lax
from jax.experimental import pallas as pl
from jax.experimental.pallas import tpu as pltpu
from jax.sharding import Mesh, PartitionSpec as P

NS_STEPS = 5
COEFFS = (3.4445, -4.775, 2.0315)
HIGH = lax.Precision.HIGH
SPLIT = (("xl", 2), ("core", 2), ("y", 4), ("xh", 2), ("z", 4))
HEAD = ("xl", "core")
CTX = ("y", "xh", "z")
SIZES = dict(SPLIT)
RING = 4
STEPS = (2, 1, 3)
F32, BF16 = jnp.float32, jnp.bfloat16
VMEM = pl.BlockSpec(memory_space=pltpu.VMEM)
SMEM = pl.BlockSpec(memory_space=pltpu.SMEM)
PARAMS = pltpu.CompilerParams(vmem_limit_bytes=50 * 2**20)


def shift(value, axis, by):
    count = SIZES[axis]
    return lax.ppermute(value, axis, [(i, (i + by) % count) for i in range(count)])


def dot(left, right, spec):
    return jnp.einsum(spec, left, right, precision=HIGH, preferred_element_type=F32)


def halves(value):
    high = value.astype(BF16)
    return high, (value - high.astype(F32)).astype(BF16)


def product(left, right, left_dim=1, right_dim=0):
    def one(a, b):
        return lax.dot_general(
            a, b, (((left_dim,), (right_dim,)), ((), ())), preferred_element_type=F32
        )

    return one(left[0], right[0]) + (one(left[0], right[1]) + one(left[1], right[0]))


def gradient_kernel(place, k_own, k_came, t_own, t_came, w1, w2, w3, *rest):
    tops, lows, grads = rest[:RING], rest[RING : 2 * RING], rest[2 * RING]
    size = w1.shape[0]
    keys = halves(jnp.concatenate([k_own[...], k_came[...]], axis=0))
    target = halves(jnp.concatenate([t_own[...], t_came[...]], axis=0))
    first = product(keys, halves(w1[...]))
    third = product(keys, halves(w3[...]))
    sigma = jax.nn.sigmoid(first)
    swish = first * sigma
    grads[1] = product(halves(swish * third), target, 0, 0)
    back = product(target, halves(w2[...]), 1, 1)
    grads[2] = product(keys, halves(back * swish), 0, 0)
    d_first = back * third * sigma * (1.0 + first * (1.0 - sigma))
    grads[0] = product(keys, halves(d_first), 0, 0)
    row = size // 2 // RING
    for d in range(RING):
        top = pl.multiple_of(((place[0] + d) & (RING - 1)) * row, row)
        low = pl.multiple_of(((place[1] + d) & (RING - 1)) * row + size // 2, row)
        tops[d][...] = grads[:, pl.ds(top, row), :]
        lows[d][...] = grads[:, pl.ds(low, row), :]


def gradients(place, keys, target, weights):
    size = weights[0].shape[0]
    rows = 2 * keys[0].shape[0]
    chunk = jax.ShapeDtypeStruct((3, size // 2 // RING, size), F32)
    out = pl.pallas_call(
        gradient_kernel,
        out_shape=[chunk] * (2 * RING),
        in_specs=[SMEM] + [VMEM] * 7,
        out_specs=[VMEM] * (2 * RING),
        scratch_shapes=[pltpu.VMEM((3, size, size), F32)],
        compiler_params=PARAMS,
        cost_estimate=pl.CostEstimate(
            flops=36 * rows * size * size, bytes_accessed=32 * size * size, transcendentals=rows * size
        ),
        name="gradients",
    )(place, *keys, *target, *weights)
    return out[:RING], out[RING:]


def update_kernel(place, eta, *refs):
    tops, lows, weights, outs = refs[:RING], refs[RING : 2 * RING], refs[8:11], refs[11:14]
    x, xh, xl, ah, al, bh, bl = refs[14:]
    size = x.shape[1]
    row, half = size // 2 // RING, size // 2
    for number, d in enumerate((0,) + STEPS):
        top = pl.multiple_of(((place[0] - d) & (RING - 1)) * row, row)
        low = pl.multiple_of(((place[1] - d) & (RING - 1)) * row + half, row)
        x[:, pl.ds(top, row), :] = tops[number][...]
        x[:, pl.ds(low, row), :] = lows[number][...]
    for m in range(3):
        g = x[m]
        scaled = g / (jnp.sqrt(jnp.sum(g * g)) + 1e-07)
        x[m] = scaled
        xh[m], xl[m] = halves(scaled)

    def part(i):
        return slice(i * half, (i + 1) * half)

    def rows(pair, m, i):
        return tuple(ref[m, part(i), :] for ref in pair)

    def columns(pair, m, j):
        return tuple(ref[m, :, part(j)] for ref in pair)

    def block(pair, m, i, j):
        return pair[0][m, part(i), part(j)].astype(F32) + pair[1][m, part(i), part(j)].astype(F32)

    def symmetric(pair, m, make):
        for i, j in ((0, 1), (0, 0), (1, 1)):
            for ref, piece in zip(pair, halves(make(i, j))):
                ref[m, part(i), part(j)] = piece
        for ref in pair:
            ref[m, part(1), part(0)] = ref[m, part(0), part(1)].T

    xs, squares, blends = (xh, xl), (ah, al), (bh, bl)

    def step(_, carry):
        for m in range(3):
            symmetric(
                squares, m, lambda i, j: product(rows(xs, m, i), rows(xs, m, j), 1, 1)
            )
        for m in range(3):
            symmetric(
                blends,
                m,
                lambda i, j: COEFFS[1] * block(squares, m, i, j)
                + COEFFS[2] * product(rows(squares, m, i), columns(squares, m, j)),
            )
        for m in range(3):
            new = COEFFS[0] * x[m] + product((bh[m], bl[m]), (xh[m], xl[m]))
            x[m] = new
            xh[m], xl[m] = halves(new)
        return carry

    lax.fori_loop(0, NS_STEPS, step, 0)
    for m in range(3):
        outs[m][...] = weights[m][...] + eta[0] * x[m]


def update(place, eta, tops, lows, weights):
    size = weights[0].shape[0]
    return pl.pallas_call(
        update_kernel,
        out_shape=[jax.ShapeDtypeStruct((size, size), F32)] * 3,
        in_specs=[SMEM, SMEM] + [VMEM] * (2 * RING + 3),
        out_specs=[VMEM] * 3,
        scratch_shapes=[pltpu.VMEM((3, size, size), F32)] + [pltpu.VMEM((3, size, size), BF16)] * 6,
        compiler_params=PARAMS,
        cost_estimate=pl.CostEstimate(
            flops=3 * 15 * 6 * size**3, bytes_accessed=36 * size * size, transcendentals=0
        ),
        name="update",
    )(place, eta, *tops, *lows, *weights)


def finish_kernel(picked, gate, gain, out):
    heads, _, size = picked.shape
    total = sum(jnp.sum(picked[h] * picked[h], axis=1, keepdims=True) for h in range(heads))
    scale = lax.rsqrt(total / (heads * size) + 1e-06)
    for h in range(heads):
        here = slice(h * size, (h + 1) * size)
        now = gate[:, here]
        out[:, here] = picked[h] * scale * gain[:, here] * (now * jax.nn.sigmoid(now))


def finish(picked, gate, gain):
    return pl.pallas_call(
        finish_kernel,
        out_shape=jax.ShapeDtypeStruct(gate.shape, F32),
        in_specs=[VMEM] * 3,
        out_specs=VMEM,
        compiler_params=PARAMS,
        cost_estimate=pl.CostEstimate(
            flops=8 * gate.size, bytes_accessed=12 * gate.size, transcendentals=gate.size
        ),
        name="finish",
    )(picked, gate, gain)


def apply_fast(queries, first_w, second_w, third_w):
    first = dot(queries, first_w, "td,de->te")
    third = dot(queries, third_w, "td,de->te")
    return dot(jax.nn.silu(first) * third, second_w, "td,de->te")


def sum_plane(tops, lows):
    top, low = tops[0], lows[0]
    came = [(shift(tops[d], "y", d), shift(lows[d], "z", d)) for d in STEPS]
    for a, b in came:
        top, low = top + a, low + b
    came = [(shift(top, "z", d), shift(low, "y", d)) for d in STEPS]
    for a, b in came:
        top, low = top + a, low + b
    came = [(shift(top, "y", d), shift(low, "z", d)) for d in STEPS]
    return [top] + [a for a, _ in came], [low] + [b for _, b in came]


def on_device(
    keys, values, queries, rates, w_first, w_second, w_third, step_size, owner_order, gate, gain
):
    size = w_first.shape[1]
    spans, rows = keys.shape[0], keys.shape[1]
    mine = lax.axis_index("xh")
    low_side = mine == 0
    heads = SIZES["xl"] * SIZES["core"]
    place = jnp.stack([lax.axis_index("y"), lax.axis_index("z")]).astype(jnp.int32)

    def sides(array):
        left, right = array[:, :size], array[:, size:]
        return jnp.where(low_side, left, right), jnp.where(low_side, right, left)

    def swapped(array):
        kept, sent = sides(array)
        return kept, shift(sent, "xh", 1)

    now_keys = swapped(keys[0])
    now_target = swapped(values[0] * rates[0][:, None])
    pieces = [queries[0]] + [
        piece for s in range(1, spans) for piece in (keys[s], values[s] * rates[s][:, None], queries[s])
    ]
    kept, sent = zip(*[sides(piece) for piece in pieces])
    order = owner_order[0]
    later, order, *first_came = lax.optimization_barrier(
        (jnp.stack(sent), order, now_keys[1], now_target[1])
    )
    now_keys, now_target = (now_keys[0], first_came[0]), (now_target[0], first_came[1])
    came = shift(later, "xh", 1)
    other = shift(order, "xh", 1)
    pairs = [(kept[n], came[n]) for n in range(len(kept))]

    weights = [jnp.where(low_side, w[0], w[1]) for w in (w_first, w_second, w_third)]
    eta = jnp.where(low_side, step_size[:1], step_size[1:])
    outputs = []
    for span in range(spans):
        if span:
            now_keys, now_target = pairs[3 * span - 2], pairs[3 * span - 1]
        tops, lows = sum_plane(*gradients(place, now_keys, now_target, weights))
        weights = update(place, eta, tops, lows, weights)
        outputs.append(apply_fast(jnp.concatenate(pairs[3 * span]), *weights))
    results = jnp.concatenate(outputs, axis=0)

    def locate(tokens, block):
        return (tokens // rows) * (2 * rows) + block * rows + tokens % rows

    here, there = locate(order, 0), locate(other, 1)
    low = jnp.where(low_side, here, there).reshape(heads, 1, -1)
    high = jnp.where(low_side, there, here).reshape(heads, 1, -1)
    index = jnp.concatenate([low, high], axis=1).reshape(-1)
    picked = jnp.take(results, index, axis=0)
    regrouped = lax.all_to_all(picked, ("xl", "core", "xh"), split_axis=0, concat_axis=0, tiled=True)
    return finish(regrouped.reshape(2 * heads, -1, size), gate[0], gain[None])[None]


def solution(mesh):
    split = Mesh(
        mesh.devices.reshape([count for _, count in SPLIT]), [name for name, _ in SPLIT]
    )
    in_specs = (
        P(None, CTX, HEAD),
        P(None, CTX, HEAD),
        P(None, CTX, HEAD),
        P(None, CTX),
        P(HEAD, None, None),
        P(HEAD, None, None),
        P(HEAD, None, None),
        P(HEAD),
        P(CTX, None),
        P(CTX, HEAD, None),
        P(),
    )
    out_specs = P(CTX, HEAD, None)
    return jax.shard_map(
        on_device, mesh=split, in_specs=in_specs, out_specs=out_specs, check_vma=False
    )
```

profile of v0, /device:TPU:1, one launch (start us, length us, event | category | flops | bytes accessed | tf_op | source)
XLA Modules:
  0.0 304.2 jit_solution(4500749961798489825)
XLA Ops:
  0.8 1.5 bitcast_multiply_fusion
  3.1 3.6 %collective-permute-start.1 = (f32[192,512]{1,0:T(8,128)S(1)}, f32[192,512]{1,0:T(8,128)}, u32[]{:S(2)}, u32[]{:S(2)}) collective-permute-start(f32[192,512]{1,0:T(8,128)S(1)} %get-tuple-element.72), channel_id=1, source_target_pairs={{0,4},{4,0},{1,5},{5,1},{2,6},{6,2},{3,7},{7,3},{8,12},{12,8},{9,1... | collective-permute-start | bytes 1179656 | tf_op jit(solution)/shard_map/ppermute | solution.py:25
  8.4 2.4 slice_bitcast_fusion.3
  10.9 2.7 select_bitcast_fusion.2.w1.refs_8_
  13.6 2.3 slice_select_fusion.5
  18.6 1.8 select_bitcast_fusion
  20.4 3.1 %collective-permute-done.k_came = f32[192,512]{1,0:T(8,128)S(1)} collective-permute-done((f32[192,512]{1,0:T(8,128)}, f32[192,512]{1,0:T(8,128)S(1)}, u32[]{:S(2)}, u32[]{:S(2)}) %collective-permute-start) | collective-permute-done | bytes 393248 | tf_op jit(solution)/shard_map/ppermute | solution.py:25
  23.5 7.3 %gradients.2 = (f32[3,64,512]{2,1,0:T(8,128)S(1)}, f32[3,64,512]{2,1,0:T(8,128)S(1)}, f32[3,64,512]{2,1,0:T(8,128)S(1)}, f32[3,64,512]{2,1,0:T(8,128)S(1)}, f32[...) custom-call(s32[2]{0:T(128)S(1)} %pad_add_fusion.1.place, ...), custom_call_target="tpu_custom_call" | custom-call | flops 3623878656 | bytes 8388608 | tf_op jit(solution)/shard_map/gradients/pallas_call | solution.py:72
  30.8 4.1 %collective-permute-start.13 = (f32[3,64,512]{2,1,0:T(8,128)S(1)}, f32[3,64,512]{2,1,0:T(8,128)S(1)}, u32[]{:S(2)}, u32[]{:S(2)}) collective-permute-start(f32[3,64,512]{2,1,0:T(8,128)S(1)} %get-tuple-element.40), channel_id=1, source_target_pairs={{0,2},{1,3},{2,0},{3,1},{4,6},{5,7},{6,4},{7,5},{8,10},{9,11},{10,... | collective-permute-start | bytes 1179656 | tf_op jit(solution)/shard_map/ppermute | solution.py:25
  35.6 1.9 collective-permute-start.15
  37.6 2.9 collective-permute-start.4
  40.9 1.9 collective-permute-done.13
  42.8 2.7 collective-permute-start.6
  45.5 7.4 %collective-permute-done.14 = f32[3,64,512]{2,1,0:T(8,128)S(1)} collective-permute-done((f32[3,64,512]{2,1,0:T(8,128)S(1)}, f32[3,64,512]{2,1,0:T(8,128)S(1)}, u32[]{:S(2)}, u32[]{:S(2)}) %collective-permute-start.14) | collective-permute-done | bytes 393248 | tf_op jit(solution)/shard_map/ppermute | solution.py:25
  53.0 3.0 collective-permute-start.16
  56.4 2.3 collective-permute-start.18
  61.0 1.7 collective-permute-start.8
  62.7 3.2 %collective-permute-done.16 = f32[3,64,512]{2,1,0:T(8,128)S(1)} collective-permute-done((f32[3,64,512]{2,1,0:T(8,128)S(1)}, f32[3,64,512]{2,1,0:T(8,128)S(1)}, u32[]{:S(2)}, u32[]{:S(2)}) %collective-permute-start.16) | collective-permute-done | bytes 393248 | tf_op jit(solution)/shard_map/ppermute | solution.py:25
  65.9 2.1 collective-permute-start.9
  68.0 7.4 %collective-permute-done.17 = f32[3,64,512]{2,1,0:T(8,128)S(1)} collective-permute-done((f32[3,64,512]{2,1,0:T(8,128)S(1)}, f32[3,64,512]{2,1,0:T(8,128)S(1)}, u32[]{:S(2)}, u32[]{:S(2)}) %collective-permute-start.17) | collective-permute-done | bytes 393248 | tf_op jit(solution)/shard_map/ppermute | solution.py:25
  76.3 1.7 collective-permute-start.20
  79.0 2.6 collective-permute-done.8
  82.5 5.9 %collective-permute-done.19.refs_5_ = f32[3,64,512]{2,1,0:T(8,128)S(1)} collective-permute-done((f32[3,64,512]{2,1,0:T(8,128)S(1)}, f32[3,64,512]{2,1,0:T(8,128)S(1)}, u32[]{:S(2)}, u32[]{:S(2)}) %collective-permute-start.19) | collective-permute-done | bytes 393248 | tf_op jit(solution)/shard_map/ppermute | solution.py:25
  88.4 1.7 collective-permute-start.12
  92.0 5.7 %collective-permute-done.20.refs_6_ = f32[3,64,512]{2,1,0:T(8,128)S(1)} collective-permute-done((f32[3,64,512]{2,1,0:T(8,128)S(1)}, f32[3,64,512]{2,1,0:T(8,128)S(1)}, u32[]{:S(2)}, u32[]{:S(2)}) %collective-permute-start.20) | collective-permute-done | bytes 393248 | tf_op jit(solution)/shard_map/ppermute | solution.py:25
  97.6 2.7 collective-permute-start.3
  100.9 37.8 %update.2 = (f32[512,512]{1,0:T(8,128)}, f32[512,512]{1,0:T(8,128)}, f32[512,512]{1,0:T(8,128)}) custom-call(s32[2]{0:T(128)S(1)} %pad_add_fusion.1.place, f32[1]{0:T(128)S(6)} %select_n.152.eta, f32[3,64,512]{2,1,0:T(8,128)S(1)} %add_add_fusion.6.refs_0_, f32[3,64,512]{2,1,0:T(8,128)S(1)} %collective-permute-done.10.refs_1_, ...), custom_call_target="tpu_custom_call" | custom-call | flops 36238786560 | bytes 9437184 | tf_op jit(solution)/shard_map/update/pallas_call | solution.py:149
  139.7 7.3 %gradients.3 = (f32[3,64,512]{2,1,0:T(8,128)S(1)}, f32[3,64,512]{2,1,0:T(8,128)S(1)}, f32[3,64,512]{2,1,0:T(8,128)S(1)}, f32[3,64,512]{2,1,0:T(8,128)S(1)}, f32[...) custom-call(s32[2]{0:T(128)S(1)} %pad_add_fusion.1.place, ...), custom_call_target="tpu_custom_call" | custom-call | flops 3623878656 | bytes 8388608 | tf_op jit(solution)/shard_map/gradients/pallas_call | solution.py:72
  149.1 1.8 collective-permute-start.33
  151.2 13.4 %collective-permute-start.22 = (f32[3,64,512]{2,1,0:T(8,128)S(1)}, f32[3,64,512]{2,1,0:T(8,128)S(1)}, u32[]{:S(2)}, u32[]{:S(2)}) collective-permute-start(f32[3,64,512]{2,1,0:T(8,128)S(1)} %get-tuple-element.47), channel_id=1, source_target_pairs={{0,16},{8,24},{16,0},{24,8},{1,17},{9,25},{17,1},{25,9},{2,18},{10... | collective-permute-start | bytes 1179656 | tf_op jit(solution)/shard_map/ppermute | solution.py:25
  164.6 3.5 %collective-permute-start.23 = (f32[3,64,512]{2,1,0:T(8,128)S(1)}, f32[3,64,512]{2,1,0:T(8,128)S(1)}, u32[]{:S(2)}, u32[]{:S(2)}) collective-permute-start(f32[3,64,512]{2,1,0:T(8,128)S(1)} %get-tuple-element.48), channel_id=1, source_target_pairs={{0,8},{8,16},{16,24},{24,0},{1,9},{9,17},{17,25},{25,1},{2,10},{10... | collective-permute-start | bytes 1179656 | tf_op jit(solution)/shard_map/ppermute | solution.py:25
  169.5 1.9 collective-permute-start.34
  171.4 1.4 collective-permute-done.22
  172.8 3.6 %collective-permute-start.36 = (f32[3,64,512]{2,1,0:T(8,128)S(1)}, f32[3,64,512]{2,1,0:T(8,128)S(1)}, u32[]{:S(2)}, u32[]{:S(2)}) collective-permute-start(f32[3,64,512]{2,1,0:T(8,128)S(1)} %add_add_fusion.1), channel_id=1, source_target_pairs={{0,24},{8,0},{16,8},{24,16},{1,25},{9,1},{17,9},{25,17},{2,26},{10... | collective-permute-start | bytes 1179656 | tf_op jit(solution)/shard_map/ppermute | solution.py:25
  176.5 11.5 %collective-permute-done.23 = f32[3,64,512]{2,1,0:T(8,128)S(1)} collective-permute-done((f32[3,64,512]{2,1,0:T(8,128)S(1)}, f32[3,64,512]{2,1,0:T(8,128)S(1)}, u32[]{:S(2)}, u32[]{:S(2)}) %collective-permute-start.23) | collective-permute-done | bytes 393248 | tf_op jit(solution)/shard_map/ppermute | solution.py:25
  191.0 10.5 %collective-permute-done.35 = f32[3,64,512]{2,1,0:T(8,128)S(1)} collective-permute-done((f32[3,64,512]{2,1,0:T(8,128)S(1)}, f32[3,64,512]{2,1,0:T(8,128)S(1)}, u32[]{:S(2)}, u32[]{:S(2)}) %collective-permute-start.35) | collective-permute-done | bytes 393248 | tf_op jit(solution)/shard_map/ppermute | solution.py:25
  203.0 2.7 collective-permute-start.39
  205.6 4.8 %collective-permute-done.26 = f32[3,64,512]{2,1,0:T(8,128)S(1)} collective-permute-done((f32[3,64,512]{2,1,0:T(8,128)S(1)}, f32[3,64,512]{2,1,0:T(8,128)S(1)}, u32[]{:S(2)}, u32[]{:S(2)}) %collective-permute-start.26) | collective-permute-done | bytes 393248 | tf_op jit(solution)/shard_map/ppermute | solution.py:25
  210.6 5.1 %collective-permute-start.29 = (f32[3,64,512]{2,1,0:T(8,128)S(1)}, f32[3,64,512]{2,1,0:T(8,128)S(1)}, u32[]{:S(2)}, u32[]{:S(2)}) collective-permute-start(f32[3,64,512]{2,1,0:T(8,128)S(1)} %add_add_fusion.2.refs_0_), channel_id=1, source_target_pairs={{0,8},{8,16},{16,24},{24,0},{1,9},{9,17},{17,25},{25,1},{2,10},{10... | collective-permute-start | bytes 1179656 | tf_op jit(solution)/shard_map/ppermute | solution.py:25
  215.7 2.7 collective-permute-start.30
  220.3 4.9 %collective-permute-done.38.refs_6_ = f32[3,64,512]{2,1,0:T(8,128)S(1)} collective-permute-done((f32[3,64,512]{2,1,0:T(8,128)S(1)}, f32[3,64,512]{2,1,0:T(8,128)S(1)}, u32[]{:S(2)}, u32[]{:S(2)}) %collective-permute-start.38) | collective-permute-done | bytes 393248 | tf_op jit(solution)/shard_map/ppermute | solution.py:25
  225.2 3.7 %collective-permute-done.29.refs_2_ = f32[3,64,512]{2,1,0:T(8,128)S(1)} collective-permute-done((f32[3,64,512]{2,1,0:T(8,128)S(1)}, f32[3,64,512]{2,1,0:T(8,128)S(1)}, u32[]{:S(2)}, u32[]{:S(2)}) %collective-permute-start.29) | collective-permute-done | bytes 393248 | tf_op jit(solution)/shard_map/ppermute | solution.py:25
  228.9 2.9 collective-permute-done.30.refs_3_
  231.8 37.8 %update.3 = (f32[512,512]{1,0:T(8,128)}, f32[512,512]{1,0:T(8,128)}, f32[512,512]{1,0:T(8,128)}) custom-call(s32[2]{0:T(128)S(1)} %pad_add_fusion.1.place, f32[1]{0:T(128)S(6)} %select_n.152.eta, f32[3,64,512]{2,1,0:T(8,128)S(1)} %add_add_fusion.2.refs_0_, f32[3,64,512]{2,1,0:T(8,128)S(1)} %collective-permute-done.28.refs_1_, ...), custom_call_target="tpu_custom_call" | custom-call | flops 36238786560 | bytes 9437184 | tf_op jit(solution)/shard_map/update/pallas_call | solution.py:149
  269.6 2.1 fusion.15
  274.0 2.2 gather_fusion
  276.4 25.9 %all_to_all.6.picked = f32[8,96,512]{2,1,0:T(8,128)S(1)} all-to-all(f32[8,96,512]{2,1,0:T(8,128)S(1)} %broadcast_select_fusion), channel_id=1, replica_groups=mesh['xl'=2,'core'=2,'y'=4,'xh'=2,'z'=4] {'xl','core','xh'}, dimensions={0} | all-to-all | bytes 3145728 | tf_op jit(solution)/shard_map/all_to_all | solution.py:257
  302.3 1.6 finish.1
  (108 shorter events, 27.6 us)
Async XLA Ops:
  3.1 17.2 %collective-permute-start.1 = (f32[192,512]{1,0:T(8,128)S(1)}, f32[192,512]{1,0:T(8,128)}, u32[]{:S(2)}, u32[]{:S(2)}) collective-permute-start(f32[192,512]{1,0:T(8,128)S(1)} %get-tuple-element.72), channel_id=1, source_target_pairs={{0,4},{4,0},{1,5},{5,1},{2,6},{6,2},{3,7},{7,3},{8,12},{12,8},{9,1... | collective-permute-start | bytes 1179656 | tf_op jit(solution)/shard_map/ppermute | solution.py:25
  7.7 15.8 %collective-permute-start = (f32[192,512]{1,0:T(8,128)}, f32[192,512]{1,0:T(8,128)S(1)}, u32[]{:S(2)}, u32[]{:S(2)}) collective-permute-start(f32[192,512]{1,0:T(8,128)} %get-tuple-element.74), channel_id=1, source_target_pairs={{0,4},{4,0},{1,5},{5,1},{2,6},{6,2},{3,7},{7,3},{8,12},{12,8},{9,1... | collective-permute-start | bytes 1179656 | tf_op jit(solution)/shard_map/ppermute | solution.py:25
  30.8 12.0 %collective-permute-start.13 = (f32[3,64,512]{2,1,0:T(8,128)S(1)}, f32[3,64,512]{2,1,0:T(8,128)S(1)}, u32[]{:S(2)}, u32[]{:S(2)}) collective-permute-start(f32[3,64,512]{2,1,0:T(8,128)S(1)} %get-tuple-element.40), channel_id=1, source_target_pairs={{0,2},{1,3},{2,0},{3,1},{4,6},{5,7},{6,4},{7,5},{8,10},{9,11},{10,... | collective-permute-start | bytes 1179656 | tf_op jit(solution)/shard_map/ppermute | solution.py:25
  34.9 18.0 %collective-permute-start.14 = (f32[3,64,512]{2,1,0:T(8,128)S(1)}, f32[3,64,512]{2,1,0:T(8,128)S(1)}, u32[]{:S(2)}, u32[]{:S(2)}) collective-permute-start(f32[3,64,512]{2,1,0:T(8,128)S(1)} %get-tuple-element.41), channel_id=1, source_target_pairs={{0,1},{1,2},{2,3},{3,0},{4,5},{5,6},{6,7},{7,4},{8,9},{9,10},{10,1... | collective-permute-start | bytes 1179656 | tf_op jit(solution)/shard_map/ppermute | solution.py:25
  35.6 17.3 %collective-permute-start.15 = (f32[3,64,512]{2,1,0:T(8,128)S(1)}, f32[3,64,512]{2,1,0:T(8,128)S(1)}, u32[]{:S(2)}, u32[]{:S(2)}) collective-permute-start(f32[3,64,512]{2,1,0:T(8,128)S(1)} %get-tuple-element.42), channel_id=1, source_target_pairs={{0,3},{1,0},{2,1},{3,2},{4,7},{5,4},{6,5},{7,6},{8,11},{9,8},{10,9... | collective-permute-start | bytes 1179656 | tf_op jit(solution)/shard_map/ppermute | solution.py:25
  37.6 18.9 %collective-permute-start.4 = (f32[3,64,512]{2,1,0:T(8,128)S(1)}, f32[3,64,512]{2,1,0:T(8,128)S(1)}, u32[]{:S(2)}, u32[]{:S(2)}) collective-permute-start(f32[3,64,512]{2,1,0:T(8,128)S(1)} %get-tuple-element.36), channel_id=1, source_target_pairs={{0,16},{8,24},{16,0},{24,8},{1,17},{9,25},{17,1},{25,9},{2,18},{10... | collective-permute-start | bytes 1179656 | tf_op jit(solution)/shard_map/ppermute | solution.py:25
  40.5 19.1 %collective-permute-start.5 = (f32[3,64,512]{2,1,0:T(8,128)S(1)}, f32[3,64,512]{2,1,0:T(8,128)S(1)}, u32[]{:S(2)}, u32[]{:S(2)}) collective-permute-start(f32[3,64,512]{2,1,0:T(8,128)S(1)} %get-tuple-element.37), channel_id=1, source_target_pairs={{0,8},{8,16},{16,24},{24,0},{1,9},{9,17},{17,25},{25,1},{2,10},{10... | collective-permute-start | bytes 1179656 | tf_op jit(solution)/shard_map/ppermute | solution.py:25
  42.8 16.8 %collective-permute-start.6 = (f32[3,64,512]{2,1,0:T(8,128)S(1)}, f32[3,64,512]{2,1,0:T(8,128)S(1)}, u32[]{:S(2)}, u32[]{:S(2)}) collective-permute-start(f32[3,64,512]{2,1,0:T(8,128)S(1)} %get-tuple-element.38), channel_id=1, source_target_pairs={{0,24},{8,0},{16,8},{24,16},{1,25},{9,1},{17,9},{25,17},{2,26},{10... | collective-permute-start | bytes 1179656 | tf_op jit(solution)/shard_map/ppermute | solution.py:25
  53.0 12.8 %collective-permute-start.16 = (f32[3,64,512]{2,1,0:T(8,128)S(1)}, f32[3,64,512]{2,1,0:T(8,128)S(1)}, u32[]{:S(2)}, u32[]{:S(2)}) collective-permute-start(f32[3,64,512]{2,1,0:T(8,128)S(1)} %add_add_fusion.5), channel_id=1, source_target_pairs={{0,16},{8,24},{16,0},{24,8},{1,17},{9,25},{17,1},{25,9},{2,18},{10... | collective-permute-start | bytes 1179656 | tf_op jit(solution)/shard_map/ppermute | solution.py:25
  56.0 19.4 %collective-permute-start.17 = (f32[3,64,512]{2,1,0:T(8,128)S(1)}, f32[3,64,512]{2,1,0:T(8,128)S(1)}, u32[]{:S(2)}, u32[]{:S(2)}) collective-permute-start(f32[3,64,512]{2,1,0:T(8,128)S(1)} %add_add_fusion.5), channel_id=1, source_target_pairs={{0,8},{8,16},{16,24},{24,0},{1,9},{9,17},{17,25},{25,1},{2,10},{10... | collective-permute-start | bytes 1179656 | tf_op jit(solution)/shard_map/ppermute | solution.py:25
  56.4 19.0 %collective-permute-start.18 = (f32[3,64,512]{2,1,0:T(8,128)S(1)}, f32[3,64,512]{2,1,0:T(8,128)S(1)}, u32[]{:S(2)}, u32[]{:S(2)}) collective-permute-start(f32[3,64,512]{2,1,0:T(8,128)S(1)} %add_add_fusion.5), channel_id=1, source_target_pairs={{0,24},{8,0},{16,8},{24,16},{1,25},{9,1},{17,9},{25,17},{2,26},{10... | collective-permute-start | bytes 1179656 | tf_op jit(solution)/shard_map/ppermute | solution.py:25
  59.7 30.3 %copy-start.11 = (f32[2]{0:T(128)S(1)}, f32[2]{0:T(128)}, u32[]{:S(2)}) copy-start(f32[2]{0:T(128)} %param.18) | copy-start | bytes 28
  59.7 18.3 %collective-permute-start.7 = (f32[3,64,512]{2,1,0:T(8,128)S(1)}, f32[3,64,512]{2,1,0:T(8,128)S(1)}, u32[]{:S(2)}, u32[]{:S(2)}) collective-permute-start(f32[3,64,512]{2,1,0:T(8,128)S(1)} %add_add_fusion.7), channel_id=1, source_target_pairs={{0,2},{1,3},{2,0},{3,1},{4,6},{5,7},{6,4},{7,5},{8,10},{9,11},{10,... | collective-permute-start | bytes 1179656 | tf_op jit(solution)/shard_map/ppermute | solution.py:25
  61.0 20.7 %collective-permute-start.8 = (f32[3,64,512]{2,1,0:T(8,128)S(1)}, f32[3,64,512]{2,1,0:T(8,128)S(1)}, u32[]{:S(2)}, u32[]{:S(2)}) collective-permute-start(f32[3,64,512]{2,1,0:T(8,128)S(1)} %add_add_fusion.7), channel_id=1, source_target_pairs={{0,1},{1,2},{2,3},{3,0},{4,5},{5,6},{6,7},{7,4},{8,9},{9,10},{10,1... | collective-permute-start | bytes 1179656 | tf_op jit(solution)/shard_map/ppermute | solution.py:25
  65.9 15.8 %collective-permute-start.9 = (f32[3,64,512]{2,1,0:T(8,128)S(1)}, f32[3,64,512]{2,1,0:T(8,128)S(1)}, u32[]{:S(2)}, u32[]{:S(2)}) collective-permute-start(f32[3,64,512]{2,1,0:T(8,128)S(1)} %add_add_fusion.7), channel_id=1, source_target_pairs={{0,3},{1,0},{2,1},{3,2},{4,7},{5,4},{6,5},{7,6},{8,11},{9,8},{10,9... | collective-permute-start | bytes 1179656 | tf_op jit(solution)/shard_map/ppermute | solution.py:25
  75.6 12.8 %collective-permute-start.19 = (f32[3,64,512]{2,1,0:T(8,128)S(1)}, f32[3,64,512]{2,1,0:T(8,128)S(1)}, u32[]{:S(2)}, u32[]{:S(2)}) collective-permute-start(f32[3,64,512]{2,1,0:T(8,128)S(1)} %add_add_fusion.4.refs_4_), channel_id=1, source_target_pairs={{0,2},{1,3},{2,0},{3,1},{4,6},{5,7},{6,4},{7,5},{8,10},{9,11},{10,... | collective-permute-start | bytes 1179656 | tf_op jit(solution)/shard_map/ppermute | solution.py:25
  76.3 21.3 %collective-permute-start.20 = (f32[3,64,512]{2,1,0:T(8,128)S(1)}, f32[3,64,512]{2,1,0:T(8,128)S(1)}, u32[]{:S(2)}, u32[]{:S(2)}) collective-permute-start(f32[3,64,512]{2,1,0:T(8,128)S(1)} %add_add_fusion.4.refs_4_), channel_id=1, source_target_pairs={{0,1},{1,2},{2,3},{3,0},{4,5},{5,6},{6,7},{7,4},{8,9},{9,10},{10,1... | collective-permute-start | bytes 1179656 | tf_op jit(solution)/shard_map/ppermute | solution.py:25
  78.0 22.4 %collective-permute-start.21 = (f32[3,64,512]{2,1,0:T(8,128)S(1)}, f32[3,64,512]{2,1,0:T(8,128)S(1)}, u32[]{:S(2)}, u32[]{:S(2)}) collective-permute-start(f32[3,64,512]{2,1,0:T(8,128)S(1)} %add_add_fusion.4.refs_4_), channel_id=1, source_target_pairs={{0,3},{1,0},{2,1},{3,2},{4,7},{5,4},{6,5},{7,6},{8,11},{9,8},{10,9... | collective-permute-start | bytes 1179656 | tf_op jit(solution)/shard_map/ppermute | solution.py:25
  81.8 19.1 %collective-permute-start.10 = (f32[3,64,512]{2,1,0:T(8,128)S(1)}, f32[3,64,512]{2,1,0:T(8,128)S(1)}, u32[]{:S(2)}, u32[]{:S(2)}) collective-permute-start(f32[3,64,512]{2,1,0:T(8,128)S(1)} %add_add_fusion.6.refs_0_), channel_id=1, source_target_pairs={{0,16},{8,24},{16,0},{24,8},{1,17},{9,25},{17,1},{25,9},{2,18},{10... | collective-permute-start | bytes 1179656 | tf_op jit(solution)/shard_map/ppermute | solution.py:25
  81.9 19.0 %collective-permute-start.11 = (f32[3,64,512]{2,1,0:T(8,128)S(1)}, f32[3,64,512]{2,1,0:T(8,128)S(1)}, u32[]{:S(2)}, u32[]{:S(2)}) collective-permute-start(f32[3,64,512]{2,1,0:T(8,128)S(1)} %add_add_fusion.6.refs_0_), channel_id=1, source_target_pairs={{0,8},{8,16},{16,24},{24,0},{1,9},{9,17},{17,25},{25,1},{2,10},{10... | collective-permute-start | bytes 1179656 | tf_op jit(solution)/shard_map/ppermute | solution.py:25
  88.4 12.5 %collective-permute-start.12 = (f32[3,64,512]{2,1,0:T(8,128)S(1)}, f32[3,64,512]{2,1,0:T(8,128)S(1)}, u32[]{:S(2)}, u32[]{:S(2)}) collective-permute-start(f32[3,64,512]{2,1,0:T(8,128)S(1)} %add_add_fusion.6.refs_0_), channel_id=1, source_target_pairs={{0,24},{8,0},{16,8},{24,16},{1,25},{9,1},{17,9},{25,17},{2,26},{10... | collective-permute-start | bytes 1179656 | tf_op jit(solution)/shard_map/ppermute | solution.py:25
  97.6 41.0 %collective-permute-start.3 = (f32[4,192,512]{2,1,0:T(8,128)S(1)}, f32[4,192,512]{2,1,0:T(8,128)S(1)}, u32[]{:S(2)}, u32[]{:S(2)}) collective-permute-start(f32[4,192,512]{2,1,0:T(8,128)S(1)} %pad_maximum_fusion), channel_id=1, source_target_pairs={{0,4},{4,0},{1,5},{5,1},{2,6},{6,2},{3,7},{7,3},{8,12},{12,8},{9,1... | collective-permute-start | bytes 4718600 | tf_op jit(solution)/shard_map/ppermute | solution.py:25
  100.4 50.5 %collective-permute-start.2 = (s32[384]{0:T(512)S(1)}, s32[384]{0:T(512)S(1)}, u32[]{:S(2)}, u32[]{:S(2)}) collective-permute-start(s32[384]{0:T(512)S(1)} %reduce), channel_id=1, source_target_pairs={{0,4},{4,0},{1,5},{5,1},{2,6},{6,2},{3,7},{7,3},{8,12},{12,8},{9,1... | collective-permute-start | bytes 4616 | tf_op jit(solution)/shard_map/ppermute | solution.py:25
  147.0 21.1 %collective-permute-start.31 = (f32[3,64,512]{2,1,0:T(8,128)S(1)}, f32[3,64,512]{2,1,0:T(8,128)}, u32[]{:S(2)}, u32[]{:S(2)}) collective-permute-start(f32[3,64,512]{2,1,0:T(8,128)S(1)} %get-tuple-element.51), channel_id=1, source_target_pairs={{0,2},{1,3},{2,0},{3,1},{4,6},{5,7},{6,4},{7,5},{8,10},{9,11},{10,... | collective-permute-start | bytes 1179656 | tf_op jit(solution)/shard_map/ppermute | solution.py:25
  148.2 19.9 %collective-permute-start.32 = (f32[3,64,512]{2,1,0:T(8,128)S(1)}, f32[3,64,512]{2,1,0:T(8,128)}, u32[]{:S(2)}, u32[]{:S(2)}) collective-permute-start(f32[3,64,512]{2,1,0:T(8,128)S(1)} %get-tuple-element.52), channel_id=1, source_target_pairs={{0,1},{1,2},{2,3},{3,0},{4,5},{5,6},{6,7},{7,4},{8,9},{9,10},{10,1... | collective-permute-start | bytes 1179656 | tf_op jit(solution)/shard_map/ppermute | solution.py:25
  149.1 19.1 %collective-permute-start.33 = (f32[3,64,512]{2,1,0:T(8,128)S(1)}, f32[3,64,512]{2,1,0:T(8,128)}, u32[]{:S(2)}, u32[]{:S(2)}) collective-permute-start(f32[3,64,512]{2,1,0:T(8,128)S(1)} %get-tuple-element.53), channel_id=1, source_target_pairs={{0,3},{1,0},{2,1},{3,2},{4,7},{5,4},{6,5},{7,6},{8,11},{9,8},{10,9... | collective-permute-start | bytes 1179656 | tf_op jit(solution)/shard_map/ppermute | solution.py:25
  151.2 21.6 %collective-permute-start.22 = (f32[3,64,512]{2,1,0:T(8,128)S(1)}, f32[3,64,512]{2,1,0:T(8,128)S(1)}, u32[]{:S(2)}, u32[]{:S(2)}) collective-permute-start(f32[3,64,512]{2,1,0:T(8,128)S(1)} %get-tuple-element.47), channel_id=1, source_target_pairs={{0,16},{8,24},{16,0},{24,8},{1,17},{9,25},{17,1},{25,9},{2,18},{10... | collective-permute-start | bytes 1179656 | tf_op jit(solution)/shard_map/ppermute | solution.py:25
  164.6 23.4 %collective-permute-start.23 = (f32[3,64,512]{2,1,0:T(8,128)S(1)}, f32[3,64,512]{2,1,0:T(8,128)S(1)}, u32[]{:S(2)}, u32[]{:S(2)}) collective-permute-start(f32[3,64,512]{2,1,0:T(8,128)S(1)} %get-tuple-element.48), channel_id=1, source_target_pairs={{0,8},{8,16},{16,24},{24,0},{1,9},{9,17},{17,25},{25,1},{2,10},{10... | collective-permute-start | bytes 1179656 | tf_op jit(solution)/shard_map/ppermute | solution.py:25
  168.1 19.8 %collective-permute-start.24 = (f32[3,64,512]{2,1,0:T(8,128)S(1)}, f32[3,64,512]{2,1,0:T(8,128)S(1)}, u32[]{:S(2)}, u32[]{:S(2)}) collective-permute-start(f32[3,64,512]{2,1,0:T(8,128)S(1)} %get-tuple-element.49), channel_id=1, source_target_pairs={{0,24},{8,0},{16,8},{24,16},{1,25},{9,1},{17,9},{25,17},{2,26},{10... | collective-permute-start | bytes 1179656 | tf_op jit(solution)/shard_map/ppermute | solution.py:25
  169.5 20.1 %collective-permute-start.34 = (f32[3,64,512]{2,1,0:T(8,128)S(1)}, f32[3,64,512]{2,1,0:T(8,128)S(1)}, u32[]{:S(2)}, u32[]{:S(2)}) collective-permute-start(f32[3,64,512]{2,1,0:T(8,128)S(1)} %add_add_fusion.1), channel_id=1, source_target_pairs={{0,16},{8,24},{16,0},{24,8},{1,17},{9,25},{17,1},{25,9},{2,18},{10... | collective-permute-start | bytes 1179656 | tf_op jit(solution)/shard_map/ppermute | solution.py:25
  171.4 30.0 %collective-permute-start.35 = (f32[3,64,512]{2,1,0:T(8,128)S(1)}, f32[3,64,512]{2,1,0:T(8,128)S(1)}, u32[]{:S(2)}, u32[]{:S(2)}) collective-permute-start(f32[3,64,512]{2,1,0:T(8,128)S(1)} %add_add_fusion.1), channel_id=1, source_target_pairs={{0,8},{8,16},{16,24},{24,0},{1,9},{9,17},{17,25},{25,1},{2,10},{10... | collective-permute-start | bytes 1179656 | tf_op jit(solution)/shard_map/ppermute | solution.py:25
  172.8 28.9 %collective-permute-start.36 = (f32[3,64,512]{2,1,0:T(8,128)S(1)}, f32[3,64,512]{2,1,0:T(8,128)S(1)}, u32[]{:S(2)}, u32[]{:S(2)}) collective-permute-start(f32[3,64,512]{2,1,0:T(8,128)S(1)} %add_add_fusion.1), channel_id=1, source_target_pairs={{0,24},{8,0},{16,8},{24,16},{1,25},{9,1},{17,9},{25,17},{2,26},{10... | collective-permute-start | bytes 1179656 | tf_op jit(solution)/shard_map/ppermute | solution.py:25
  188.0 14.0 %copy-start.2 = (f32[192,512]{1,0:T(8,128)S(1)}, f32[192,512]{1,0:T(8,128)}, u32[]{:S(2)}) copy-start(f32[192,512]{1,0:T(8,128)} %get-tuple-element.57) | copy-start | bytes 1179652
  188.0 14.0 %copy-start.4 = (f32[192,512]{1,0:T(8,128)S(1)}, f32[192,512]{1,0:T(8,128)}, u32[]{:S(2)}) copy-start(f32[192,512]{1,0:T(8,128)} %get-tuple-element.90) | copy-start | bytes 1179652
  188.0 14.0 %copy-start.8 = (f32[512,512]{1,0:T(8,128)S(1)}, f32[512,512]{1,0:T(8,128)}, u32[]{:S(2)}) copy-start(f32[512,512]{1,0:T(8,128)} %get-tuple-element.43.w1.refs_8_) | copy-start | bytes 3145732
  188.1 14.8 %collective-permute-start.25 = (f32[3,64,512]{2,1,0:T(8,128)S(1)}, f32[3,64,512]{2,1,0:T(8,128)S(1)}, u32[]{:S(2)}, u32[]{:S(2)}) collective-permute-start(f32[3,64,512]{2,1,0:T(8,128)S(1)} %add_add_fusion.3), channel_id=1, source_target_pairs={{0,2},{1,3},{2,0},{3,1},{4,6},{5,7},{6,4},{7,5},{8,10},{9,11},{10,... | collective-permute-start | bytes 1179656 | tf_op jit(solution)/shard_map/ppermute | solution.py:25
  188.2 22.2 %collective-permute-start.26 = (f32[3,64,512]{2,1,0:T(8,128)S(1)}, f32[3,64,512]{2,1,0:T(8,128)S(1)}, u32[]{:S(2)}, u32[]{:S(2)}) collective-permute-start(f32[3,64,512]{2,1,0:T(8,128)S(1)} %add_add_fusion.3), channel_id=1, source_target_pairs={{0,1},{1,2},{2,3},{3,0},{4,5},{5,6},{6,7},{7,4},{8,9},{9,10},{10,1... | collective-permute-start | bytes 1179656 | tf_op jit(solution)/shard_map/ppermute | solution.py:25
  189.7 20.7 %collective-permute-start.27 = (f32[3,64,512]{2,1,0:T(8,128)S(1)}, f32[3,64,512]{2,1,0:T(8,128)S(1)}, u32[]{:S(2)}, u32[]{:S(2)}) collective-permute-start(f32[3,64,512]{2,1,0:T(8,128)S(1)} %add_add_fusion.3), channel_id=1, source_target_pairs={{0,3},{1,0},{2,1},{3,2},{4,7},{5,4},{6,5},{7,6},{8,11},{9,8},{10,9... | collective-permute-start | bytes 1179656 | tf_op jit(solution)/shard_map/ppermute | solution.py:25
  201.9 13.9 %collective-permute-start.37 = (f32[3,64,512]{2,1,0:T(8,128)S(1)}, f32[3,64,512]{2,1,0:T(8,128)S(1)}, u32[]{:S(2)}, u32[]{:S(2)}) collective-permute-start(f32[3,64,512]{2,1,0:T(8,128)S(1)} %add_add_fusion.refs_4_), channel_id=1, source_target_pairs={{0,2},{1,3},{2,0},{3,1},{4,6},{5,7},{6,4},{7,5},{8,10},{9,11},{10,... | collective-permute-start | bytes 1179656 | tf_op jit(solution)/shard_map/ppermute | solution.py:25
  202.9 15.6 %copy-start.9 = (f32[512,512]{1,0:T(8,128)S(1)}, f32[512,512]{1,0:T(8,128)}, u32[]{:S(2)}) copy-start(f32[512,512]{1,0:T(8,128)} %get-tuple-element.44.w3.refs_10_) | copy-start | bytes 3145732
  202.9 22.3 %collective-permute-start.38 = (f32[3,64,512]{2,1,0:T(8,128)S(1)}, f32[3,64,512]{2,1,0:T(8,128)S(1)}, u32[]{:S(2)}, u32[]{:S(2)}) collective-permute-start(f32[3,64,512]{2,1,0:T(8,128)S(1)} %add_add_fusion.refs_4_), channel_id=1, source_target_pairs={{0,1},{1,2},{2,3},{3,0},{4,5},{5,6},{6,7},{7,4},{8,9},{9,10},{10,1... | collective-permute-start | bytes 1179656 | tf_op jit(solution)/shard_map/ppermute | solution.py:25
  203.0 22.2 %collective-permute-start.39 = (f32[3,64,512]{2,1,0:T(8,128)S(1)}, f32[3,64,512]{2,1,0:T(8,128)S(1)}, u32[]{:S(2)}, u32[]{:S(2)}) collective-permute-start(f32[3,64,512]{2,1,0:T(8,128)S(1)} %add_add_fusion.refs_4_), channel_id=1, source_target_pairs={{0,3},{1,0},{2,1},{3,2},{4,7},{5,4},{6,5},{7,6},{8,11},{9,8},{10,9... | collective-permute-start | bytes 1179656 | tf_op jit(solution)/shard_map/ppermute | solution.py:25
  210.5 14.6 %collective-permute-start.28 = (f32[3,64,512]{2,1,0:T(8,128)S(1)}, f32[3,64,512]{2,1,0:T(8,128)S(1)}, u32[]{:S(2)}, u32[]{:S(2)}) collective-permute-start(f32[3,64,512]{2,1,0:T(8,128)S(1)} %add_add_fusion.2.refs_0_), channel_id=1, source_target_pairs={{0,16},{8,24},{16,0},{24,8},{1,17},{9,25},{17,1},{25,9},{2,18},{10... | collective-permute-start | bytes 1179656 | tf_op jit(solution)/shard_map/ppermute | solution.py:25
  210.6 18.2 %collective-permute-start.29 = (f32[3,64,512]{2,1,0:T(8,128)S(1)}, f32[3,64,512]{2,1,0:T(8,128)S(1)}, u32[]{:S(2)}, u32[]{:S(2)}) collective-permute-start(f32[3,64,512]{2,1,0:T(8,128)S(1)} %add_add_fusion.2.refs_0_), channel_id=1, source_target_pairs={{0,8},{8,16},{16,24},{24,0},{1,9},{9,17},{17,25},{25,1},{2,10},{10... | collective-permute-start | bytes 1179656 | tf_op jit(solution)/shard_map/ppermute | solution.py:25
  215.7 16.0 %collective-permute-start.30 = (f32[3,64,512]{2,1,0:T(8,128)S(1)}, f32[3,64,512]{2,1,0:T(8,128)S(1)}, u32[]{:S(2)}, u32[]{:S(2)}) collective-permute-start(f32[3,64,512]{2,1,0:T(8,128)S(1)} %add_add_fusion.2.refs_0_), channel_id=1, source_target_pairs={{0,24},{8,0},{16,8},{24,16},{1,25},{9,1},{17,9},{25,17},{2,26},{10... | collective-permute-start | bytes 1179656 | tf_op jit(solution)/shard_map/ppermute | solution.py:25
  220.3 49.3 %copy-start.3 = (f32[192,512]{1,0:T(8,128)S(1)}, f32[192,512]{1,0:T(8,128)}, u32[]{:S(2)}) copy-start(f32[192,512]{1,0:T(8,128)} %get-tuple-element.88) | copy-start | bytes 1179652
  276.4 25.9 %copy-start = (f32[1,96,4096]{2,1,0:T(8,128)S(1)}, f32[1,96,4096]{2,1,0:T(8,128)}, u32[]{:S(2)}) copy-start(f32[1,96,4096]{2,1,0:T(8,128)} %param.20) | copy-start | bytes 4718596
  276.4 25.9 %copy-start.1 = (f32[4096]{0:T(1024)S(1)}, f32[4096]{0:T(1024)}, u32[]{:S(2)}) copy-start(f32[4096]{0:T(1024)} %param.21) | copy-start | bytes 49156
  (7 other events, 22.5 us)
where the time goes:
time: 307 us; the launch traced here: 304 us
  Pallas kernels  91.9 us (30%)
  waiting for transfers between devices  79.4 us (26%)
  starting transfers between devices  75.4 us (25%)
  blocking collectives  25.9 us (8%)
  other arithmetic  13.9 us (5%)
  local copies, waits for them, and re-layouts  9.33 us (3%)
  matrix products  6.56 us (2%)
    ppermute x40, waiting for transfers between devices, shift(): lax.ppermute(value, axis, [(i, (i + by) % count) for i in range(count)])  79.4 us
    pallas_call x2, Pallas kernels, update(): pl.pallas_call(update_kernel, out_shape=[jax.ShapeDtypeStruct((size, size...  75.6 us
    ppermute x40, starting transfers between devices, shift(): lax.ppermute(value, axis, [(i, (i + by) % count) for i in range(count)])  75.4 us
    all_to_all x1, blocking collectives, on_device(): lax.all_to_all(picked, ('xl', 'core', 'xh'), split_axis=0, concat_axis=0,...  25.9 us
    pallas_call x2, Pallas kernels, gradients(): pl.pallas_call(gradient_kernel, out_shape=[chunk] * (2 * RING), in_specs=...  14.6 us
    dot_general x6, matrix products, dot(): jnp.einsum(spec, left, right, precision=HIGH, preferred_element_type=F32)  6.56 us
  transfers between devices with their start and end apart: 40, of which 18 were waited for; matrix products, arithmetic and copies ran while one was open for 6% of the time, Pallas kernels for 15%

commit v1 on v0

--- a/solution.py
+++ b/solution.py
@@ -43,11 +43,9 @@
     return one(left[0], right[0]) + (one(left[0], right[1]) + one(left[1], right[0]))
 
 
-def gradient_kernel(place, k_own, k_came, t_own, t_came, w1, w2, w3, *rest):
-    tops, lows, grads = rest[:RING], rest[RING : 2 * RING], rest[2 * RING]
+def gradient_chunks(place, keys, target, w1, w2, w3, tops, lows, grads):
     size = w1.shape[0]
-    keys = halves(jnp.concatenate([k_own[...], k_came[...]], axis=0))
-    target = halves(jnp.concatenate([t_own[...], t_came[...]], axis=0))
+    keys, target = halves(keys), halves(target)
     first = product(keys, halves(w1[...]))
     third = product(keys, halves(w3[...]))
     sigma = jax.nn.sigmoid(first)
@@ -65,99 +63,184 @@
         lows[d][...] = grads[:, pl.ds(low, row), :]
 
 
+def add_updates(place, eta, updates, weights, outs):
+    kind = place[0] + place[1]
+    for m in range(3):
+        for e in range(RING):
+
+            @pl.when(((m - kind) & (RING - 1)) == e)
+            def _(m=m, e=e):
+                outs[m][...] = weights[m][...] + eta[0] * updates[e][...]
+
+
+def first_kernel(place, k_own, k_came, t_own, t_came, w1, w2, w3, *rest):
+    keys = jnp.concatenate([k_own[...], k_came[...]], axis=0)
+    target = jnp.concatenate([t_own[...], t_came[...]], axis=0)
+    gradient_chunks(place, keys, target, w1, w2, w3, rest[:RING], rest[RING : 2 * RING], rest[2 * RING])
+
+
+def next_kernel(place, eta, k_own, k_came, t_own, t_came, *refs):
+    updates, weights, outs = refs[:RING], refs[4:7], refs[7:10]
+    tops, lows, grads = refs[10 : 10 + RING], refs[10 + RING : 10 + 2 * RING], refs[10 + 2 * RING]
+    add_updates(place, eta, updates, weights, outs)
+    keys = jnp.concatenate([k_own[...], k_came[...]], axis=0)
+    target = jnp.concatenate([t_own[...], t_came[...]], axis=0)
+    gradient_chunks(place, keys, target, *outs, tops, lows, grads)
+
+
+def last_kernel(place, eta, q_own, q_came, *refs):
+    updates, weights, result, held = refs[:RING], refs[4:7], refs[7], refs[8:]
+    add_updates(place, eta, updates, weights, held)
+    queries = halves(jnp.concatenate([q_own[...], q_came[...]], axis=0))
+    first = product(queries, halves(held[0][...]))
+    third = product(queries, halves(held[2][...]))
+    result[...] = product(halves(first * jax.nn.sigmoid(first) * third), halves(held[1][...]))
+
+
+def gradient_cost(rows, size):
+    return pl.CostEstimate(
+        flops=36 * rows * size * size, bytes_accessed=32 * size * size, transcendentals=rows * size
+    )
+
+
 def gradients(place, keys, target, weights):
     size = weights[0].shape[0]
-    rows = 2 * keys[0].shape[0]
     chunk = jax.ShapeDtypeStruct((3, size // 2 // RING, size), F32)
     out = pl.pallas_call(
-        gradient_kernel,
+        first_kernel,
         out_shape=[chunk] * (2 * RING),
         in_specs=[SMEM] + [VMEM] * 7,
         out_specs=[VMEM] * (2 * RING),
         scratch_shapes=[pltpu.VMEM((3, size, size), F32)],
         compiler_params=PARAMS,
-        cost_estimate=pl.CostEstimate(
-            flops=36 * rows * size * size, bytes_accessed=32 * size * size, transcendentals=rows * size
-        ),
+        cost_estimate=gradient_cost(2 * keys[0].shape[0], size),
         name="gradients",
     )(place, *keys, *target, *weights)
     return out[:RING], out[RING:]
 
 
-def update_kernel(place, eta, *refs):
-    tops, lows, weights, outs = refs[:RING], refs[RING : 2 * RING], refs[8:11], refs[11:14]
-    x, xh, xl, ah, al, bh, bl = refs[14:]
-    size = x.shape[1]
+def update_and_gradients(place, eta, keys, target, updates, weights):
+    size = weights[0].shape[0]
+    chunk = jax.ShapeDtypeStruct((3, size // 2 // RING, size), F32)
+    square = jax.ShapeDtypeStruct((size, size), F32)
+    out = pl.pallas_call(
+        next_kernel,
+        out_shape=[square] * 3 + [chunk] * (2 * RING),
+        in_specs=[SMEM, SMEM] + [VMEM] * (RING + 7),
+        out_specs=[VMEM] * (3 + 2 * RING),
+        scratch_shapes=[pltpu.VMEM((3, size, size), F32)],
+        compiler_params=PARAMS,
+        cost_estimate=gradient_cost(2 * keys[0].shape[0], size),
+        name="update_and_gradients",
+    )(place, eta, *keys, *target, *updates, *weights)
+    return out[:3], out[3 : 3 + RING], out[3 + RING :]
+
+
+def update_and_apply(place, eta, queries, updates, weights):
+    size = weights[0].shape[0]
+    rows = 2 * queries[0].shape[0]
+    return pl.pallas_call(
+        last_kernel,
+        out_shape=jax.ShapeDtypeStruct((rows, size), F32),
+        in_specs=[SMEM, SMEM] + [VMEM] * (RING + 5),
+        out_specs=VMEM,
+        scratch_shapes=[pltpu.VMEM((size, size), F32)] * 3,
+        compiler_params=PARAMS,
+        cost_estimate=pl.CostEstimate(
+            flops=18 * rows * size * size, bytes_accessed=32 * size * size, transcendentals=rows * size
+        ),
+        name="update_and_apply",
+    )(place, eta, *queries, *updates, *weights)
+
+
+def pick_kernel(place, own, *refs):
+    came, outs = refs[: RING - 1], refs[RING - 1 :]
+    kind = place[0] + place[1]
+    for d in range(RING):
+        matrix = jnp.minimum((kind + d) & (RING - 1), 2)
+        outs[d][...] = own[matrix] + (came[0][matrix] + (came[1][matrix] + came[2][matrix]))
+
+
+def pick(place, own, came):
+    chunk = jax.ShapeDtypeStruct(own.shape[1:], F32)
+    return pl.pallas_call(
+        pick_kernel,
+        out_shape=[chunk] * RING,
+        in_specs=[SMEM] + [VMEM] * RING,
+        out_specs=[VMEM] * RING,
+        compiler_params=PARAMS,
+        cost_estimate=pl.CostEstimate(
+            flops=4 * own.size, bytes_accessed=22 * own.size, transcendentals=0
+        ),
+        name="pick",
+    )(place, own, *came)
+
+
+def orthogonal_kernel(place, *refs):
+    chunks, out, (x, xh, xl, ah, al, bh, bl) = refs[:RING], refs[4], refs[5:]
+    size = x.shape[0]
     row, half = size // 2 // RING, size // 2
-    for number, d in enumerate((0,) + STEPS):
+    for d in range(RING):
         top = pl.multiple_of(((place[0] - d) & (RING - 1)) * row, row)
-        low = pl.multiple_of(((place[1] - d) & (RING - 1)) * row + half, row)
-        x[:, pl.ds(top, row), :] = tops[number][...]
-        x[:, pl.ds(low, row), :] = lows[number][...]
-    for m in range(3):
-        g = x[m]
-        scaled = g / (jnp.sqrt(jnp.sum(g * g)) + 1e-07)
-        x[m] = scaled
-        xh[m], xl[m] = halves(scaled)
+        low = pl.multiple_of(((place[1] + d) & (RING - 1)) * row + half, row)
+        x[pl.ds(top, row), :] = chunks[d][0]
+        x[pl.ds(low, row), :] = chunks[d][1]
+    g = x[...]
+    scaled = g / (jnp.sqrt(jnp.sum(g * g)) + 1e-07)
+    x[...] = scaled
+    xh[...], xl[...] = halves(scaled)
 
     def part(i):
         return slice(i * half, (i + 1) * half)
 
-    def rows(pair, m, i):
-        return tuple(ref[m, part(i), :] for ref in pair)
-
-    def columns(pair, m, j):
-        return tuple(ref[m, :, part(j)] for ref in pair)
-
-    def block(pair, m, i, j):
-        return pair[0][m, part(i), part(j)].astype(F32) + pair[1][m, part(i), part(j)].astype(F32)
-
-    def symmetric(pair, m, make):
+    def rows(pair, i):
+        return tuple(ref[part(i), :] for ref in pair)
+
+    def columns(pair, j):
+        return tuple(ref[:, part(j)] for ref in pair)
+
+    def block(pair, i, j):
+        return pair[0][part(i), part(j)].astype(F32) + pair[1][part(i), part(j)].astype(F32)
+
+    def symmetric(pair, make):
         for i, j in ((0, 1), (0, 0), (1, 1)):
             for ref, piece in zip(pair, halves(make(i, j))):
-                ref[m, part(i), part(j)] = piece
+                ref[part(i), part(j)] = piece
         for ref in pair:
-            ref[m, part(1), part(0)] = ref[m, part(0), part(1)].T
+            ref[part(1), part(0)] = ref[part(0), part(1)].T
 
     xs, squares, blends = (xh, xl), (ah, al), (bh, bl)
 
     def step(_, carry):
-        for m in range(3):
-            symmetric(
-                squares, m, lambda i, j: product(rows(xs, m, i), rows(xs, m, j), 1, 1)
-            )
-        for m in range(3):
-            symmetric(
-                blends,
-                m,
-                lambda i, j: COEFFS[1] * block(squares, m, i, j)
-                + COEFFS[2] * product(rows(squares, m, i), columns(squares, m, j)),
-            )
-        for m in range(3):
-            new = COEFFS[0] * x[m] + product((bh[m], bl[m]), (xh[m], xl[m]))
-            x[m] = new
-            xh[m], xl[m] = halves(new)
+        symmetric(squares, lambda i, j: product(rows(xs, i), rows(xs, j), 1, 1))
+        symmetric(
+            blends,
+            lambda i, j: COEFFS[1] * block(squares, i, j)
+            + COEFFS[2] * product(rows(squares, i), columns(squares, j)),
+        )
+        new = COEFFS[0] * x[...] + product((bh[...], bl[...]), (xh[...], xl[...]))
+        x[...] = new
+        xh[...], xl[...] = halves(new)
         return carry
 
     lax.fori_loop(0, NS_STEPS, step, 0)
-    for m in range(3):
-        outs[m][...] = weights[m][...] + eta[0] * x[m]
-
-
-def update(place, eta, tops, lows, weights):
-    size = weights[0].shape[0]
+    out[...] = x[...]
+
+
+def orthogonal(place, chunks):
+    size = chunks[0].shape[-1]
     return pl.pallas_call(
-        update_kernel,
-        out_shape=[jax.ShapeDtypeStruct((size, size), F32)] * 3,
-        in_specs=[SMEM, SMEM] + [VMEM] * (2 * RING + 3),
-        out_specs=[VMEM] * 3,
-        scratch_shapes=[pltpu.VMEM((3, size, size), F32)] + [pltpu.VMEM((3, size, size), BF16)] * 6,
+        orthogonal_kernel,
+        out_shape=jax.ShapeDtypeStruct((size, size), F32),
+        in_specs=[SMEM] + [VMEM] * RING,
+        out_specs=VMEM,
+        scratch_shapes=[pltpu.VMEM((size, size), F32)] + [pltpu.VMEM((size, size), BF16)] * 6,
         compiler_params=PARAMS,
         cost_estimate=pl.CostEstimate(
-            flops=3 * 15 * 6 * size**3, bytes_accessed=36 * size * size, transcendentals=0
+            flops=15 * 6 * size**3, bytes_accessed=8 * size * size, transcendentals=0
         ),
-        name="update",
-    )(place, eta, *tops, *lows, *weights)
+        name="orthogonal",
+    )(place, *chunks)
 
 
 def finish_kernel(picked, gate, gain, out):
@@ -190,16 +273,32 @@
     return dot(jax.nn.silu(first) * third, second_w, "td,de->te")
 
 
-def sum_plane(tops, lows):
+def plane_shift(value, dy, dz, used=lambda y, z: True):
+    pairs = [
+        (y * RING + z, (y + dy) % RING * RING + (z + dz) % RING)
+        for y in range(RING)
+        for z in range(RING)
+        if used(y, z)
+    ]
+    return lax.ppermute(value, ("y", "z"), pairs)
+
+
+def sum_to_diagonals(place, tops, lows):
+    top_came = [plane_shift(tops[d], d, 0) for d in STEPS]
+    low_came = [plane_shift(lows[d], 0, d) for d in STEPS]
+    tops, lows = pick(place, tops[0], top_came), pick(place, lows[0], low_came)
     top, low = tops[0], lows[0]
-    came = [(shift(tops[d], "y", d), shift(lows[d], "z", d)) for d in STEPS]
-    for a, b in came:
-        top, low = top + a, low + b
-    came = [(shift(top, "z", d), shift(low, "y", d)) for d in STEPS]
-    for a, b in came:
-        top, low = top + a, low + b
-    came = [(shift(top, "y", d), shift(low, "z", d)) for d in STEPS]
-    return [top] + [a for a, _ in came], [low] + [b for _, b in came]
+    for d in STEPS:
+        top = top + plane_shift(tops[d], 0, d)
+        low = low + plane_shift(lows[d], d, 0)
+    held = jnp.stack([top, low])
+    return [held] + [plane_shift(held, d, -d) for d in range(1, RING)]
+
+
+def share(update):
+    used = lambda y, z: (y + z) % RING < 3
+    opposite = plane_shift(update, RING // 2, 0, used)
+    return [update, plane_shift(update, 0, -1, used), opposite, plane_shift(update, 0, 1, used)]
 
 
 def on_device(
@@ -238,12 +337,16 @@
     weights = [jnp.where(low_side, w[0], w[1]) for w in (w_first, w_second, w_third)]
     eta = jnp.where(low_side, step_size[:1], step_size[1:])
     outputs = []
+    chunks = gradients(place, now_keys, now_target, weights)
     for span in range(spans):
-        if span:
-            now_keys, now_target = pairs[3 * span - 2], pairs[3 * span - 1]
-        tops, lows = sum_plane(*gradients(place, now_keys, now_target, weights))
-        weights = update(place, eta, tops, lows, weights)
-        outputs.append(apply_fast(jnp.concatenate(pairs[3 * span]), *weights))
+        updates = share(orthogonal(place, sum_to_diagonals(place, *chunks)))
+        now = pairs[3 * span]
+        if span + 1 < spans:
+            later = pairs[3 * span + 1], pairs[3 * span + 2]
+            weights, *chunks = update_and_gradients(place, eta, *later, updates, weights)
+            outputs.append(apply_fast(jnp.concatenate(now), *weights))
+        else:
+            outputs.append(update_and_apply(place, eta, now, updates, weights))
     results = jnp.concatenate(outputs, axis=0)
 
     def locate(tokens, block):

time: 307 us -> 295 us (0.961); the launches traced: 304 us -> 289 us
  Pallas kernels: 91.9 us -> 58 us
  starting transfers between devices: 75.4 us -> 91 us
  waiting for transfers between devices: 79.4 us -> 85.5 us
  matrix products: 6.56 us -> 2.64 us
  other arithmetic: 13.9 us -> 10.4 us
    ppermute x0 -> x36, starting transfers between devices: none -> 81.1 us  [plane_shift(): return lax.ppermute(value, ('y', 'z'), pairs)]
    ppermute x0 -> x36, waiting for transfers between devices: none -> 80.9 us  [plane_shift(): return lax.ppermute(value, ('y', 'z'), pairs)]
    ppermute x40 -> x4, waiting for transfers between devices: 79.4 us -> 4.52 us  [shift(): lax.ppermute(value, axis, [(i, (i + by) % count) for i in range(count)])]
    ppermute x40 -> x4, starting transfers between devices: 75.4 us -> 9.92 us  [shift(): lax.ppermute(value, axis, [(i, (i + by) % count) for i in range(count)])]
    pallas_call x4 -> x9, Pallas kernels: 90.2 us -> 56.3 us  [the longest x2 30.2 us: orthogonal(): pl.pallas_call(orthogonal_kernel, out_shape=jax.ShapeDtypeStruct((size, s...]
    dot_general x6 -> x3, matrix products: 6.56 us -> 2.64 us  [dot(): jnp.einsum(spec, left, right, precision=HIGH, preferred_element_type=F32)]
  transfers between devices with their start and end apart: 40 -> 40, of which waited for: 18 -> 21; matrix products, arithmetic and copies ran while one was open for 6% -> 6% of each run, Pallas kernels for 15% -> 6%
where the time goes in v1:
time: 295 us; the launch traced here: 289 us
  starting transfers between devices  91 us (31%)
  waiting for transfers between devices  85.5 us (29%)
  Pallas kernels  58 us (20%)
  blocking collectives  27.5 us (9%)
  local copies, waits for them, and re-layouts  12.2 us (4%)
  other arithmetic  10.4 us (4%)
    ppermute x36, starting transfers between devices, plane_shift(): return lax.ppermute(value, ('y', 'z'), pairs)  81.1 us
    ppermute x36, waiting for transfers between devices, plane_shift(): return lax.ppermute(value, ('y', 'z'), pairs)  80.9 us
    pallas_call x2, Pallas kernels, orthogonal(): pl.pallas_call(orthogonal_kernel, out_shape=jax.ShapeDtypeStruct((size, s...  30.2 us
    all_to_all x1, blocking collectives, on_device(): lax.all_to_all(picked, ('xl', 'core', 'xh'), split_axis=0, concat_axis=0,...  27.5 us
    pallas_call x1, Pallas kernels, update_and_gradients(): pl.pallas_call(next_kernel, out_shape=[square] * 3 + [chunk] * (2 * RING)...  10.5 us
    ppermute x4, starting transfers between devices, shift(): lax.ppermute(value, axis, [(i, (i + by) % count) for i in range(count)])  9.92 us
    pallas_call x1, Pallas kernels, gradients(): pl.pallas_call(first_kernel, out_shape=[chunk] * (2 * RING), in_specs=[SM...  7.31 us
  transfers between devices with their start and end apart: 40, of which 21 were waited for; matrix products, arithmetic and copies ran while one was open for 6% of the time, Pallas kernels for 6%

profile of v1, /device:TPU:1, one launch (start us, length us, event | category | flops | bytes accessed | tf_op | source)
XLA Modules:
  0.0 289.1 jit_solution(2795782295735474549)
XLA Ops:
  2.4 3.6 %collective-permute-start = (f32[192,512]{1,0:T(8,128)}, f32[192,512]{1,0:T(8,128)S(1)}, u32[]{:S(2)}, u32[]{:S(2)}) collective-permute-start(f32[192,512]{1,0:T(8,128)} %get-tuple-element.98), channel_id=1, source_target_pairs={{0,4},{4,0},{1,5},{5,1},{2,6},{6,2},{3,7},{7,3},{8,12},{12,8},{9,1... | collective-permute-start | bytes 1179656 | tf_op jit(solution)/shard_map/ppermute | solution.py:25
  7.8 2.4 slice_bitcast_fusion.3
  10.2 2.8 select_bitcast_fusion.2.w1.refs_4_
  16.7 1.8 select_bitcast_fusion
  18.5 4.5 %collective-permute-done.1.t_came = f32[192,512]{1,0:T(8,128)} collective-permute-done((f32[192,512]{1,0:T(8,128)}, f32[192,512]{1,0:T(8,128)}, u32[]{:S(2)}, u32[]{:S(2)}) %collective-permute-start.1) | collective-permute-done | bytes 393248 | tf_op jit(solution)/shard_map/ppermute | solution.py:25
  23.0 7.3 %gradients.1 = (f32[3,64,512]{2,1,0:T(8,128)S(1)}, f32[3,64,512]{2,1,0:T(8,128)S(1)}, f32[3,64,512]{2,1,0:T(8,128)S(1)}, f32[3,64,512]{2,1,0:T(8,128)S(1)}, f32[...) custom-call(s32[2]{0:T(128)S(1)} %pad_add_fusion.1.place, ...), custom_call_target="tpu_custom_call" | custom-call | flops 3623878656 | bytes 8388608 | tf_op jit(solution)/shard_map/gradients/pallas_call | solution.py:109
  30.4 4.1 %collective-permute-start.10 = (f32[3,64,512]{2,1,0:T(8,128)S(1)}, f32[3,64,512]{2,1,0:T(8,128)S(1)}, u32[]{:S(2)}, u32[]{:S(2)}) collective-permute-start(f32[3,64,512]{2,1,0:T(8,128)S(1)} %get-tuple-element.57), channel_id=1, source_target_pairs={{0,2},{1,3},{2,0},{3,1},{8,10},{9,11},{10,8},{11,9},{16,18},{17,19... | collective-permute-start | bytes 1179656 | tf_op jit(solution)/shard_map/ppermute | solution.py:283
  35.2 1.9 collective-permute-start.12
  37.1 2.9 %collective-permute-start.4 = (f32[3,64,512]{2,1,0:T(8,128)S(1)}, f32[3,64,512]{2,1,0:T(8,128)S(1)}, u32[]{:S(2)}, u32[]{:S(2)}) collective-permute-start(f32[3,64,512]{2,1,0:T(8,128)S(1)} %get-tuple-element.49), channel_id=1, source_target_pairs={{0,16},{1,17},{2,18},{3,19},{8,24},{9,25},{10,26},{11,27},{16,0},{... | collective-permute-start | bytes 1179656 | tf_op jit(solution)/shard_map/ppermute | solution.py:283
  40.4 1.9 collective-permute-done.10.refs_0_
  42.4 2.7 collective-permute-start.6
  45.1 7.3 %collective-permute-done.11.refs_1_ = f32[3,64,512]{2,1,0:T(8,128)S(1)} collective-permute-done((f32[3,64,512]{2,1,0:T(8,128)S(1)}, f32[3,64,512]{2,1,0:T(8,128)S(1)}, u32[]{:S(2)}, u32[]{:S(2)}) %collective-permute-start.11) | collective-permute-done | bytes 393248 | tf_op jit(solution)/shard_map/ppermute | solution.py:283
  53.1 2.8 collective-permute-start.15
  58.7 2.7 collective-permute-start.9
  62.7 1.8 collective-permute-done.14
  64.5 3.8 %collective-permute-done.8 = f32[64,512]{1,0:T(8,128)S(1)} collective-permute-done((f32[64,512]{1,0:T(8,128)S(1)}, f32[64,512]{1,0:T(8,128)S(1)}, u32[]{:S(2)}, u32[]{:S(2)}) %collective-permute-start.8) | collective-permute-done | bytes 131104 | tf_op jit(solution)/shard_map/ppermute | solution.py:283
  68.4 2.6 collective-permute-start.16
  71.0 2.8 collective-permute-start.18
  73.8 2.9 %collective-permute-start.3 = (f32[4,192,512]{2,1,0:T(8,128)S(1)}, f32[4,192,512]{2,1,0:T(8,128)S(1)}, u32[]{:S(2)}, u32[]{:S(2)}) collective-permute-start(f32[4,192,512]{2,1,0:T(8,128)S(1)} %pad_maximum_fusion), channel_id=1, source_target_pairs={{0,4},{4,0},{1,5},{5,1},{2,6},{6,2},{3,7},{7,3},{8,12},{12,8},{9,1... | collective-permute-start | bytes 4718600 | tf_op jit(solution)/shard_map/ppermute | solution.py:25
  77.4 5.4 %collective-permute-done.17.refs_2_ = f32[2,64,512]{2,1,0:T(8,128)S(1)} collective-permute-done((f32[2,64,512]{2,1,0:T(8,128)S(1)}, f32[2,64,512]{2,1,0:T(8,128)S(1)}, u32[]{:S(2)}, u32[]{:S(2)}) %collective-permute-start.17) | collective-permute-done | bytes 262176 | tf_op jit(solution)/shard_map/ppermute | solution.py:283
  82.8 1.9 collective-permute-done.18.refs_3_
  84.7 15.1 %orthogonal.2.refs_0_ = f32[512,512]{1,0:T(8,128)S(1)} custom-call(s32[2]{0:T(128)S(1)} %pad_add_fusion.1.place, f32[2,64,512]{2,1,0:T(8,128)S(1)} %pad_maximum_fusion.5.refs_0_, f32[2,64,512]{2,1,0:T(8,128)S(1)} %collective-permute-done.16.refs_1_, f32[2,64,512]{2,1,0:T(8,128)S(1)} %collective-permute-done.17.refs_2_, ...), custom_call_target="tpu_custom_call" | custom-call | flops 12079595520 | bytes 2097152 | tf_op jit(solution)/shard_map/orthogonal/pallas_call | solution.py:232
  99.9 3.2 %collective-permute-start.19 = (f32[512,512]{1,0:T(8,128)S(1)}, f32[512,512]{1,0:T(8,128)S(1)}, u32[]{:S(2)}, u32[]{:S(2)}) collective-permute-start(f32[512,512]{1,0:T(8,128)S(1)} %orthogonal.2.refs_0_), channel_id=1, source_target_pairs={{0,3},{1,0},{2,1},{8,11},{9,8},{11,10},{16,19},{18,17},{19,18},{25... | collective-permute-start | bytes 3145736 | tf_op jit(solution)/shard_map/ppermute | solution.py:283
  103.1 4.9 %collective-permute-start.20 = (f32[512,512]{1,0:T(8,128)S(1)}, f32[512,512]{1,0:T(8,128)S(1)}, u32[]{:S(2)}, u32[]{:S(2)}) collective-permute-start(f32[512,512]{1,0:T(8,128)S(1)} %orthogonal.2.refs_0_), channel_id=1, source_target_pairs={{0,16},{1,17},{2,18},{8,24},{9,25},{11,27},{16,0},{18,2},{19,3},{2... | collective-permute-start | bytes 3145736 | tf_op jit(solution)/shard_map/ppermute | solution.py:283
  112.3 9.0 %collective-permute-done.19.refs_1_ = f32[512,512]{1,0:T(8,128)S(1)} collective-permute-done((f32[512,512]{1,0:T(8,128)S(1)}, f32[512,512]{1,0:T(8,128)S(1)}, u32[]{:S(2)}, u32[]{:S(2)}) %collective-permute-start.19) | collective-permute-done | bytes 1048608 | tf_op jit(solution)/shard_map/ppermute | solution.py:283
  121.3 6.1 %collective-permute-done.20.refs_2_ = f32[512,512]{1,0:T(8,128)S(1)} collective-permute-done((f32[512,512]{1,0:T(8,128)S(1)}, f32[512,512]{1,0:T(8,128)S(1)}, u32[]{:S(2)}, u32[]{:S(2)}) %collective-permute-start.20) | collective-permute-done | bytes 1048608 | tf_op jit(solution)/shard_map/ppermute | solution.py:283
  129.7 10.5 %update_and_gradients.1 = (f32[512,512]{1,0:T(8,128)}, f32[512,512]{1,0:T(8,128)}, f32[512,512]{1,0:T(8,128)}, f32[3,64,512]{2,1,0:T(8,128)S(1)}, f32[3,64,512]{...) custom-call(s32[2]{0:T(128)S(1)} %pad_add_fusion.1.place, ...), custom_call_target="tpu_custom_call" | custom-call | flops 3623878656 | bytes 8388608 | tf_op jit(solution)/shard_map/update_and_gradients/pallas_call | solution.py:126
  140.2 2.2 collective-permute-start.29
  142.5 2.3 collective-permute-start.30
  145.8 3.0 %collective-permute-start.23 = (f32[3,64,512]{2,1,0:T(8,128)S(1)}, f32[3,64,512]{2,1,0:T(8,128)S(1)}, u32[]{:S(2)}, u32[]{:S(2)}) collective-permute-start(f32[3,64,512]{2,1,0:T(8,128)S(1)} %get-tuple-element.69), channel_id=1, source_target_pairs={{0,8},{1,9},{2,10},{3,11},{8,16},{9,17},{10,18},{11,19},{16,24},{1... | collective-permute-start | bytes 1179656 | tf_op jit(solution)/shard_map/ppermute | solution.py:283
  148.8 4.4 %collective-permute-start.24 = (f32[3,64,512]{2,1,0:T(8,128)S(1)}, f32[3,64,512]{2,1,0:T(8,128)S(1)}, u32[]{:S(2)}, u32[]{:S(2)}) collective-permute-start(f32[3,64,512]{2,1,0:T(8,128)S(1)} %get-tuple-element.70), channel_id=1, source_target_pairs={{0,24},{1,25},{2,26},{3,27},{8,0},{9,1},{10,2},{11,3},{16,8},{17,9... | collective-permute-start | bytes 1179656 | tf_op jit(solution)/shard_map/ppermute | solution.py:283
  153.2 7.1 %collective-permute-done.29.refs_1_ = f32[3,64,512]{2,1,0:T(8,128)S(1)} collective-permute-done((f32[3,64,512]{2,1,0:T(8,128)S(1)}, f32[3,64,512]{2,1,0:T(8,128)S(1)}, u32[]{:S(2)}, u32[]{:S(2)}) %collective-permute-start.29) | collective-permute-done | bytes 393248 | tf_op jit(solution)/shard_map/ppermute | solution.py:283
  160.3 2.7 collective-permute-start.2
  164.3 4.6 %collective-permute-start.33 = (f32[64,512]{1,0:T(8,128)}, f32[64,512]{1,0:T(8,128)}, u32[]{:S(2)}, u32[]{:S(2)}) collective-permute-start(f32[64,512]{1,0:T(8,128)} %get-tuple-element.82), channel_id=1, source_target_pairs={{0,24},{1,25},{2,26},{3,27},{8,0},{9,1},{10,2},{11,3},{16,8},{17,9... | collective-permute-start | bytes 393224 | tf_op jit(solution)/shard_map/ppermute | solution.py:283
  170.0 11.0 %collective-permute-start.31 = (f32[64,512]{1,0:T(8,128)S(1)}, f32[64,512]{1,0:T(8,128)}, u32[]{:S(2)}, u32[]{:S(2)}) collective-permute-start(f32[64,512]{1,0:T(8,128)S(1)} %get-tuple-element.80), channel_id=1, source_target_pairs={{0,16},{1,17},{2,18},{3,19},{8,24},{9,25},{10,26},{11,27},{16,0},{... | collective-permute-start | bytes 393224 | tf_op jit(solution)/shard_map/ppermute | solution.py:283
  187.0 2.8 collective-permute-done.25
  191.1 3.3 %collective-permute-start.35 = (f32[2,64,512]{2,1,0:T(8,128)S(1)}, f32[2,64,512]{2,1,0:T(8,128)S(1)}, u32[]{:S(2)}, u32[]{:S(2)}) collective-permute-start(f32[2,64,512]{2,1,0:T(8,128)S(1)} %pad_maximum_fusion.6.refs_0_), channel_id=1, source_target_pairs={{0,18},{1,19},{2,16},{3,17},{8,26},{9,27},{10,24},{11,25},{16,2},{... | collective-permute-start | bytes 786440 | tf_op jit(solution)/shard_map/ppermute | solution.py:283
  194.5 2.8 collective-permute-done.34.refs_1_
  197.3 7.8 %collective-permute-done.35.refs_2_ = f32[2,64,512]{2,1,0:T(8,128)S(1)} collective-permute-done((f32[2,64,512]{2,1,0:T(8,128)S(1)}, f32[2,64,512]{2,1,0:T(8,128)S(1)}, u32[]{:S(2)}, u32[]{:S(2)}) %collective-permute-start.35) | collective-permute-done | bytes 262176 | tf_op jit(solution)/shard_map/ppermute | solution.py:283
  206.0 15.1 %orthogonal.3.refs_0_ = f32[512,512]{1,0:T(8,128)S(1)} custom-call(s32[2]{0:T(128)S(1)} %pad_add_fusion.1.place, f32[2,64,512]{2,1,0:T(8,128)S(1)} %pad_maximum_fusion.6.refs_0_, f32[2,64,512]{2,1,0:T(8,128)S(1)} %collective-permute-done.34.refs_1_, f32[2,64,512]{2,1,0:T(8,128)S(1)} %collective-permute-done.35.refs_2_, ...), custom_call_target="tpu_custom_call" | custom-call | flops 12079595520 | bytes 2097152 | tf_op jit(solution)/shard_map/orthogonal/pallas_call | solution.py:232
  221.2 5.0 %collective-permute-start.37 = (f32[512,512]{1,0:T(8,128)S(1)}, f32[512,512]{1,0:T(8,128)S(1)}, u32[]{:S(2)}, u32[]{:S(2)}) collective-permute-start(f32[512,512]{1,0:T(8,128)S(1)} %orthogonal.3.refs_0_), channel_id=1, source_target_pairs={{0,3},{1,0},{2,1},{8,11},{9,8},{11,10},{16,19},{18,17},{19,18},{25... | collective-permute-start | bytes 3145736 | tf_op jit(solution)/shard_map/ppermute | solution.py:283
  226.2 1.9 collective-permute-start.38
  232.6 12.9 %collective-permute-done.37.refs_1_ = f32[512,512]{1,0:T(8,128)S(1)} collective-permute-done((f32[512,512]{1,0:T(8,128)S(1)}, f32[512,512]{1,0:T(8,128)S(1)}, u32[]{:S(2)}, u32[]{:S(2)}) %collective-permute-start.37) | collective-permute-done | bytes 1048608 | tf_op jit(solution)/shard_map/ppermute | solution.py:283
  245.4 5.3 %collective-permute-done.38.refs_2_ = f32[512,512]{1,0:T(8,128)S(1)} collective-permute-done((f32[512,512]{1,0:T(8,128)S(1)}, f32[512,512]{1,0:T(8,128)S(1)}, u32[]{:S(2)}, u32[]{:S(2)}) %collective-permute-start.38) | collective-permute-done | bytes 1048608 | tf_op jit(solution)/shard_map/ppermute | solution.py:283
  252.1 5.1 %update_and_apply.1 = f32[384,512]{1,0:T(8,128)S(1)} custom-call(s32[2]{0:T(128)S(1)} %pad_add_fusion.1.place, f32[1]{0:T(128)S(6)} %select_n.152.eta, f32[192,512]{1,0:T(8,128)S(1)} %get-tuple-element.104.q_own, f32[192,512]{1,0:T(8,128)S(1)} %get-tuple-element.84.q_came, f32[512,512]{1,0:T(8,128)S(1)} %orthogonal.3.refs_0_, ...), custom_call_target="tpu_custom_call" | custom-call | flops 1811939328 | bytes 8388608 | tf_op jit(solution)/shard_map/update_and_apply/pallas_call | solution.py:142
  257.3 2.2 gather_fusion
  259.7 27.5 %all_to_all.6.picked = f32[8,96,512]{2,1,0:T(8,128)S(1)} all-to-all(f32[8,96,512]{2,1,0:T(8,128)S(1)} %broadcast_select_fusion), channel_id=1, replica_groups=mesh['xl'=2,'core'=2,'y'=4,'xh'=2,'z'=4] {'xl','core','xh'}, dimensions={0} | all-to-all | bytes 3145728 | tf_op jit(solution)/shard_map/all_to_all | solution.py:360
  287.2 1.6 finish.1
  (118 shorter events, 37.4 us)
Async XLA Ops:
  2.4 16.2 %collective-permute-start = (f32[192,512]{1,0:T(8,128)}, f32[192,512]{1,0:T(8,128)S(1)}, u32[]{:S(2)}, u32[]{:S(2)}) collective-permute-start(f32[192,512]{1,0:T(8,128)} %get-tuple-element.98), channel_id=1, source_target_pairs={{0,4},{4,0},{1,5},{5,1},{2,6},{6,2},{3,7},{7,3},{8,12},{12,8},{9,1... | collective-permute-start | bytes 1179656 | tf_op jit(solution)/shard_map/ppermute | solution.py:25
  7.1 15.9 %collective-permute-start.1 = (f32[192,512]{1,0:T(8,128)}, f32[192,512]{1,0:T(8,128)}, u32[]{:S(2)}, u32[]{:S(2)}) collective-permute-start(f32[192,512]{1,0:T(8,128)} %get-tuple-element.96), channel_id=1, source_target_pairs={{0,4},{4,0},{1,5},{5,1},{2,6},{6,2},{3,7},{7,3},{8,12},{12,8},{9,1... | collective-permute-start | bytes 1179656 | tf_op jit(solution)/shard_map/ppermute | solution.py:25
  30.4 12.0 %collective-permute-start.10 = (f32[3,64,512]{2,1,0:T(8,128)S(1)}, f32[3,64,512]{2,1,0:T(8,128)S(1)}, u32[]{:S(2)}, u32[]{:S(2)}) collective-permute-start(f32[3,64,512]{2,1,0:T(8,128)S(1)} %get-tuple-element.57), channel_id=1, source_target_pairs={{0,2},{1,3},{2,0},{3,1},{8,10},{9,11},{10,8},{11,9},{16,18},{17,19... | collective-permute-start | bytes 1179656 | tf_op jit(solution)/shard_map/ppermute | solution.py:283
  34.4 18.0 %collective-permute-start.11 = (f32[3,64,512]{2,1,0:T(8,128)S(1)}, f32[3,64,512]{2,1,0:T(8,128)S(1)}, u32[]{:S(2)}, u32[]{:S(2)}) collective-permute-start(f32[3,64,512]{2,1,0:T(8,128)S(1)} %get-tuple-element.58), channel_id=1, source_target_pairs={{0,1},{1,2},{2,3},{3,0},{8,9},{9,10},{10,11},{11,8},{16,17},{17,18... | collective-permute-start | bytes 1179656 | tf_op jit(solution)/shard_map/ppermute | solution.py:283
  35.2 17.3 %collective-permute-start.12 = (f32[3,64,512]{2,1,0:T(8,128)S(1)}, f32[3,64,512]{2,1,0:T(8,128)S(1)}, u32[]{:S(2)}, u32[]{:S(2)}) collective-permute-start(f32[3,64,512]{2,1,0:T(8,128)S(1)} %get-tuple-element.59), channel_id=1, source_target_pairs={{0,3},{1,0},{2,1},{3,2},{8,11},{9,8},{10,9},{11,10},{16,19},{17,16... | collective-permute-start | bytes 1179656 | tf_op jit(solution)/shard_map/ppermute | solution.py:283
  37.1 18.8 %collective-permute-start.4 = (f32[3,64,512]{2,1,0:T(8,128)S(1)}, f32[3,64,512]{2,1,0:T(8,128)S(1)}, u32[]{:S(2)}, u32[]{:S(2)}) collective-permute-start(f32[3,64,512]{2,1,0:T(8,128)S(1)} %get-tuple-element.49), channel_id=1, source_target_pairs={{0,16},{1,17},{2,18},{3,19},{8,24},{9,25},{10,26},{11,27},{16,0},{... | collective-permute-start | bytes 1179656 | tf_op jit(solution)/shard_map/ppermute | solution.py:283
  40.0 18.0 %collective-permute-start.5 = (f32[3,64,512]{2,1,0:T(8,128)S(1)}, f32[3,64,512]{2,1,0:T(8,128)S(1)}, u32[]{:S(2)}, u32[]{:S(2)}) collective-permute-start(f32[3,64,512]{2,1,0:T(8,128)S(1)} %get-tuple-element.50), channel_id=1, source_target_pairs={{0,8},{1,9},{2,10},{3,11},{8,16},{9,17},{10,18},{11,19},{16,24},{1... | collective-permute-start | bytes 1179656 | tf_op jit(solution)/shard_map/ppermute | solution.py:283
  42.4 15.7 %collective-permute-start.6 = (f32[3,64,512]{2,1,0:T(8,128)S(1)}, f32[3,64,512]{2,1,0:T(8,128)S(1)}, u32[]{:S(2)}, u32[]{:S(2)}) collective-permute-start(f32[3,64,512]{2,1,0:T(8,128)S(1)} %get-tuple-element.51), channel_id=1, source_target_pairs={{0,24},{1,25},{2,26},{3,27},{8,0},{9,1},{10,2},{11,3},{16,8},{17,9... | collective-permute-start | bytes 1179656 | tf_op jit(solution)/shard_map/ppermute | solution.py:283
  53.1 8.3 %collective-permute-start.15 = (f32[64,512]{1,0:T(8,128)S(1)}, f32[64,512]{1,0:T(8,128)S(1)}, u32[]{:S(2)}, u32[]{:S(2)}) collective-permute-start(f32[64,512]{1,0:T(8,128)S(1)} %get-tuple-element.63), channel_id=1, source_target_pairs={{0,24},{1,25},{2,26},{3,27},{8,0},{9,1},{10,2},{11,3},{16,8},{17,9... | collective-permute-start | bytes 393224 | tf_op jit(solution)/shard_map/ppermute | solution.py:283
  55.9 8.6 %collective-permute-start.14 = (f32[64,512]{1,0:T(8,128)S(1)}, f32[64,512]{1,0:T(8,128)S(1)}, u32[]{:S(2)}, u32[]{:S(2)}) collective-permute-start(f32[64,512]{1,0:T(8,128)S(1)} %get-tuple-element.62), channel_id=1, source_target_pairs={{0,8},{1,9},{2,10},{3,11},{8,16},{9,17},{10,18},{11,19},{16,24},{1... | collective-permute-start | bytes 393224 | tf_op jit(solution)/shard_map/ppermute | solution.py:283
  55.9 8.6 %collective-permute-start.13 = (f32[64,512]{1,0:T(8,128)S(1)}, f32[64,512]{1,0:T(8,128)S(1)}, u32[]{:S(2)}, u32[]{:S(2)}) collective-permute-start(f32[64,512]{1,0:T(8,128)S(1)} %get-tuple-element.61), channel_id=1, source_target_pairs={{0,16},{1,17},{2,18},{3,19},{8,24},{9,25},{10,26},{11,27},{16,0},{... | collective-permute-start | bytes 393224 | tf_op jit(solution)/shard_map/ppermute | solution.py:283
  58.7 5.8 %collective-permute-start.9 = (f32[64,512]{1,0:T(8,128)S(1)}, f32[64,512]{1,0:T(8,128)S(1)}, u32[]{:S(2)}, u32[]{:S(2)}) collective-permute-start(f32[64,512]{1,0:T(8,128)S(1)} %get-tuple-element.55), channel_id=1, source_target_pairs={{0,3},{1,0},{2,1},{3,2},{8,11},{9,8},{10,9},{11,10},{16,19},{17,16... | collective-permute-start | bytes 393224 | tf_op jit(solution)/shard_map/ppermute | solution.py:283
  61.4 6.9 %collective-permute-start.8 = (f32[64,512]{1,0:T(8,128)S(1)}, f32[64,512]{1,0:T(8,128)S(1)}, u32[]{:S(2)}, u32[]{:S(2)}) collective-permute-start(f32[64,512]{1,0:T(8,128)S(1)} %get-tuple-element.54), channel_id=1, source_target_pairs={{0,1},{1,2},{2,3},{3,0},{8,9},{9,10},{10,11},{11,8},{16,17},{17,18... | collective-permute-start | bytes 393224 | tf_op jit(solution)/shard_map/ppermute | solution.py:283
  61.4 6.9 %collective-permute-start.7 = (f32[64,512]{1,0:T(8,128)S(1)}, f32[64,512]{1,0:T(8,128)S(1)}, u32[]{:S(2)}, u32[]{:S(2)}) collective-permute-start(f32[64,512]{1,0:T(8,128)S(1)} %get-tuple-element.53), channel_id=1, source_target_pairs={{0,2},{1,3},{2,0},{3,1},{8,10},{9,11},{10,8},{11,9},{16,18},{17,19... | collective-permute-start | bytes 393224 | tf_op jit(solution)/shard_map/ppermute | solution.py:283
  68.4 41.0 %copy-start.15 = (f32[2]{0:T(128)S(1)}, f32[2]{0:T(128)}, u32[]{:S(2)}) copy-start(f32[2]{0:T(128)} %param.18) | copy-start | bytes 28
  68.4 9.0 %collective-permute-start.16 = (f32[2,64,512]{2,1,0:T(8,128)S(1)}, f32[2,64,512]{2,1,0:T(8,128)S(1)}, u32[]{:S(2)}, u32[]{:S(2)}) collective-permute-start(f32[2,64,512]{2,1,0:T(8,128)S(1)} %pad_maximum_fusion.5.refs_0_), channel_id=1, source_target_pairs={{0,11},{1,8},{2,9},{3,10},{8,19},{9,16},{10,17},{11,18},{16,27},{1... | collective-permute-start | bytes 786440 | tf_op jit(solution)/shard_map/ppermute | solution.py:283
  71.0 11.8 %collective-permute-start.17 = (f32[2,64,512]{2,1,0:T(8,128)S(1)}, f32[2,64,512]{2,1,0:T(8,128)S(1)}, u32[]{:S(2)}, u32[]{:S(2)}) collective-permute-start(f32[2,64,512]{2,1,0:T(8,128)S(1)} %pad_maximum_fusion.5.refs_0_), channel_id=1, source_target_pairs={{0,18},{1,19},{2,16},{3,17},{8,26},{9,27},{10,24},{11,25},{16,2},{... | collective-permute-start | bytes 786440 | tf_op jit(solution)/shard_map/ppermute | solution.py:283
  71.0 13.7 %collective-permute-start.18 = (f32[2,64,512]{2,1,0:T(8,128)S(1)}, f32[2,64,512]{2,1,0:T(8,128)S(1)}, u32[]{:S(2)}, u32[]{:S(2)}) collective-permute-start(f32[2,64,512]{2,1,0:T(8,128)S(1)} %pad_maximum_fusion.5.refs_0_), channel_id=1, source_target_pairs={{0,25},{1,26},{2,27},{3,24},{8,1},{9,2},{10,3},{11,0},{16,9},{17,1... | collective-permute-start | bytes 786440 | tf_op jit(solution)/shard_map/ppermute | solution.py:283
  73.8 37.5 %collective-permute-start.3 = (f32[4,192,512]{2,1,0:T(8,128)S(1)}, f32[4,192,512]{2,1,0:T(8,128)S(1)}, u32[]{:S(2)}, u32[]{:S(2)}) collective-permute-start(f32[4,192,512]{2,1,0:T(8,128)S(1)} %pad_maximum_fusion), channel_id=1, source_target_pairs={{0,4},{4,0},{1,5},{5,1},{2,6},{6,2},{3,7},{7,3},{8,12},{12,8},{9,1... | collective-permute-start | bytes 4718600 | tf_op jit(solution)/shard_map/ppermute | solution.py:25
  99.8 12.5 %copy-start.2 = (f32[512,512]{1,0:T(8,128)}, f32[512,512]{1,0:T(8,128)S(1)}, u32[]{:S(2)}) copy-start(f32[512,512]{1,0:T(8,128)S(1)} %orthogonal.2.refs_0_) | copy-start | bytes 3145732
  99.9 21.5 %collective-permute-start.19 = (f32[512,512]{1,0:T(8,128)S(1)}, f32[512,512]{1,0:T(8,128)S(1)}, u32[]{:S(2)}, u32[]{:S(2)}) collective-permute-start(f32[512,512]{1,0:T(8,128)S(1)} %orthogonal.2.refs_0_), channel_id=1, source_target_pairs={{0,3},{1,0},{2,1},{8,11},{9,8},{11,10},{16,19},{18,17},{19,18},{25... | collective-permute-start | bytes 3145736 | tf_op jit(solution)/shard_map/ppermute | solution.py:283
  103.1 24.4 %collective-permute-start.20 = (f32[512,512]{1,0:T(8,128)S(1)}, f32[512,512]{1,0:T(8,128)S(1)}, u32[]{:S(2)}, u32[]{:S(2)}) collective-permute-start(f32[512,512]{1,0:T(8,128)S(1)} %orthogonal.2.refs_0_), channel_id=1, source_target_pairs={{0,16},{1,17},{2,18},{8,24},{9,25},{11,27},{16,0},{18,2},{19,3},{2... | collective-permute-start | bytes 3145736 | tf_op jit(solution)/shard_map/ppermute | solution.py:283
  108.0 20.8 %collective-permute-start.21 = (f32[512,512]{1,0:T(8,128)S(1)}, f32[512,512]{1,0:T(8,128)S(1)}, u32[]{:S(2)}, u32[]{:S(2)}) collective-permute-start(f32[512,512]{1,0:T(8,128)S(1)} %orthogonal.2.refs_0_), channel_id=1, source_target_pairs={{0,1},{1,2},{2,3},{8,9},{9,10},{11,8},{16,17},{18,19},{19,16},{25,... | collective-permute-start | bytes 3145736 | tf_op jit(solution)/shard_map/ppermute | solution.py:283
  140.2 8.6 %collective-permute-start.28 = (f32[3,64,512]{2,1,0:T(8,128)S(1)}, f32[3,64,512]{2,1,0:T(8,128)S(1)}, u32[]{:S(2)}, u32[]{:S(2)}) collective-permute-start(f32[3,64,512]{2,1,0:T(8,128)S(1)} %get-tuple-element.76), channel_id=1, source_target_pairs={{0,2},{1,3},{2,0},{3,1},{8,10},{9,11},{10,8},{11,9},{16,18},{17,19... | collective-permute-start | bytes 1179656 | tf_op jit(solution)/shard_map/ppermute | solution.py:283
  140.2 20.0 %collective-permute-start.29 = (f32[3,64,512]{2,1,0:T(8,128)S(1)}, f32[3,64,512]{2,1,0:T(8,128)S(1)}, u32[]{:S(2)}, u32[]{:S(2)}) collective-permute-start(f32[3,64,512]{2,1,0:T(8,128)S(1)} %get-tuple-element.77), channel_id=1, source_target_pairs={{0,1},{1,2},{2,3},{3,0},{8,9},{9,10},{10,11},{11,8},{16,17},{17,18... | collective-permute-start | bytes 1179656 | tf_op jit(solution)/shard_map/ppermute | solution.py:283
  142.5 20.5 %collective-permute-start.30 = (f32[3,64,512]{2,1,0:T(8,128)S(1)}, f32[3,64,512]{2,1,0:T(8,128)S(1)}, u32[]{:S(2)}, u32[]{:S(2)}) collective-permute-start(f32[3,64,512]{2,1,0:T(8,128)S(1)} %get-tuple-element.78), channel_id=1, source_target_pairs={{0,3},{1,0},{2,1},{3,2},{8,11},{9,8},{10,9},{11,10},{16,19},{17,16... | collective-permute-start | bytes 1179656 | tf_op jit(solution)/shard_map/ppermute | solution.py:283
  144.8 25.2 %collective-permute-start.22 = (f32[3,64,512]{2,1,0:T(8,128)S(1)}, f32[3,64,512]{2,1,0:T(8,128)S(1)}, u32[]{:S(2)}, u32[]{:S(2)}) collective-permute-start(f32[3,64,512]{2,1,0:T(8,128)S(1)} %get-tuple-element.68), channel_id=1, source_target_pairs={{0,16},{1,17},{2,18},{3,19},{8,24},{9,25},{10,26},{11,27},{16,0},{... | collective-permute-start | bytes 1179656 | tf_op jit(solution)/shard_map/ppermute | solution.py:283
  145.8 35.4 %collective-permute-start.23 = (f32[3,64,512]{2,1,0:T(8,128)S(1)}, f32[3,64,512]{2,1,0:T(8,128)S(1)}, u32[]{:S(2)}, u32[]{:S(2)}) collective-permute-start(f32[3,64,512]{2,1,0:T(8,128)S(1)} %get-tuple-element.69), channel_id=1, source_target_pairs={{0,8},{1,9},{2,10},{3,11},{8,16},{9,17},{10,18},{11,19},{16,24},{1... | collective-permute-start | bytes 1179656 | tf_op jit(solution)/shard_map/ppermute | solution.py:283
  148.8 32.4 %collective-permute-start.24 = (f32[3,64,512]{2,1,0:T(8,128)S(1)}, f32[3,64,512]{2,1,0:T(8,128)S(1)}, u32[]{:S(2)}, u32[]{:S(2)}) collective-permute-start(f32[3,64,512]{2,1,0:T(8,128)S(1)} %get-tuple-element.70), channel_id=1, source_target_pairs={{0,24},{1,25},{2,26},{3,27},{8,0},{9,1},{10,2},{11,3},{16,8},{17,9... | collective-permute-start | bytes 1179656 | tf_op jit(solution)/shard_map/ppermute | solution.py:283
  160.3 8.6 %collective-permute-start.2 = (s32[384]{0:T(512)S(1)}, s32[384]{0:T(512)S(1)}, u32[]{:S(2)}, u32[]{:S(2)}) collective-permute-start(s32[384]{0:T(512)S(1)} %reduce), channel_id=1, source_target_pairs={{0,4},{4,0},{1,5},{5,1},{2,6},{6,2},{3,7},{7,3},{8,12},{12,8},{9,1... | collective-permute-start | bytes 4616 | tf_op jit(solution)/shard_map/ppermute | solution.py:25
  164.3 19.1 %collective-permute-start.33 = (f32[64,512]{1,0:T(8,128)}, f32[64,512]{1,0:T(8,128)}, u32[]{:S(2)}, u32[]{:S(2)}) collective-permute-start(f32[64,512]{1,0:T(8,128)} %get-tuple-element.82), channel_id=1, source_target_pairs={{0,24},{1,25},{2,26},{3,27},{8,0},{9,1},{10,2},{11,3},{16,8},{17,9... | collective-permute-start | bytes 393224 | tf_op jit(solution)/shard_map/ppermute | solution.py:283
  168.9 15.6 %collective-permute-start.32 = (f32[64,512]{1,0:T(8,128)S(1)}, f32[64,512]{1,0:T(8,128)}, u32[]{:S(2)}, u32[]{:S(2)}) collective-permute-start(f32[64,512]{1,0:T(8,128)S(1)} %get-tuple-element.81), channel_id=1, source_target_pairs={{0,8},{1,9},{2,10},{3,11},{8,16},{9,17},{10,18},{11,19},{16,24},{1... | collective-permute-start | bytes 393224 | tf_op jit(solution)/shard_map/ppermute | solution.py:283
  170.0 14.5 %collective-permute-start.31 = (f32[64,512]{1,0:T(8,128)S(1)}, f32[64,512]{1,0:T(8,128)}, u32[]{:S(2)}, u32[]{:S(2)}) collective-permute-start(f32[64,512]{1,0:T(8,128)S(1)} %get-tuple-element.80), channel_id=1, source_target_pairs={{0,16},{1,17},{2,18},{3,19},{8,24},{9,25},{10,26},{11,27},{16,0},{... | collective-permute-start | bytes 393224 | tf_op jit(solution)/shard_map/ppermute | solution.py:283
  181.9 4.3 %collective-permute-start.27 = (f32[64,512]{1,0:T(8,128)S(1)}, f32[64,512]{1,0:T(8,128)S(1)}, u32[]{:S(2)}, u32[]{:S(2)}) collective-permute-start(f32[64,512]{1,0:T(8,128)S(1)} %get-tuple-element.74), channel_id=1, source_target_pairs={{0,3},{1,0},{2,1},{3,2},{8,11},{9,8},{10,9},{11,10},{16,19},{17,16... | collective-permute-start | bytes 393224 | tf_op jit(solution)/shard_map/ppermute | solution.py:283
  181.9 5.1 %collective-permute-start.26 = (f32[64,512]{1,0:T(8,128)S(1)}, f32[64,512]{1,0:T(8,128)S(1)}, u32[]{:S(2)}, u32[]{:S(2)}) collective-permute-start(f32[64,512]{1,0:T(8,128)S(1)} %get-tuple-element.73), channel_id=1, source_target_pairs={{0,1},{1,2},{2,3},{3,0},{8,9},{9,10},{10,11},{11,8},{16,17},{17,18... | collective-permute-start | bytes 393224 | tf_op jit(solution)/shard_map/ppermute | solution.py:283
  183.4 6.5 %collective-permute-start.25 = (f32[64,512]{1,0:T(8,128)S(1)}, f32[64,512]{1,0:T(8,128)S(1)}, u32[]{:S(2)}, u32[]{:S(2)}) collective-permute-start(f32[64,512]{1,0:T(8,128)S(1)} %get-tuple-element.72), channel_id=1, source_target_pairs={{0,2},{1,3},{2,0},{3,1},{8,10},{9,11},{10,8},{11,9},{16,18},{17,19... | collective-permute-start | bytes 393224 | tf_op jit(solution)/shard_map/ppermute | solution.py:283
  189.9 7.4 %collective-permute-start.34 = (f32[2,64,512]{2,1,0:T(8,128)S(1)}, f32[2,64,512]{2,1,0:T(8,128)S(1)}, u32[]{:S(2)}, u32[]{:S(2)}) collective-permute-start(f32[2,64,512]{2,1,0:T(8,128)S(1)} %pad_maximum_fusion.6.refs_0_), channel_id=1, source_target_pairs={{0,11},{1,8},{2,9},{3,10},{8,19},{9,16},{10,17},{11,18},{16,27},{1... | collective-permute-start | bytes 786440 | tf_op jit(solution)/shard_map/ppermute | solution.py:283
  191.1 14.0 %collective-permute-start.35 = (f32[2,64,512]{2,1,0:T(8,128)S(1)}, f32[2,64,512]{2,1,0:T(8,128)S(1)}, u32[]{:S(2)}, u32[]{:S(2)}) collective-permute-start(f32[2,64,512]{2,1,0:T(8,128)S(1)} %pad_maximum_fusion.6.refs_0_), channel_id=1, source_target_pairs={{0,18},{1,19},{2,16},{3,17},{8,26},{9,27},{10,24},{11,25},{16,2},{... | collective-permute-start | bytes 786440 | tf_op jit(solution)/shard_map/ppermute | solution.py:283
  194.4 11.7 %collective-permute-start.36 = (f32[2,64,512]{2,1,0:T(8,128)S(1)}, f32[2,64,512]{2,1,0:T(8,128)S(1)}, u32[]{:S(2)}, u32[]{:S(2)}) collective-permute-start(f32[2,64,512]{2,1,0:T(8,128)S(1)} %pad_maximum_fusion.6.refs_0_), channel_id=1, source_target_pairs={{0,25},{1,26},{2,27},{3,24},{8,1},{9,2},{10,3},{11,0},{16,9},{17,1... | collective-permute-start | bytes 786440 | tf_op jit(solution)/shard_map/ppermute | solution.py:283
  194.5 35.0 %copy-start.4 = (f32[512,512]{1,0:T(8,128)S(1)}, f32[512,512]{1,0:T(8,128)}, u32[]{:S(2)}) copy-start(f32[512,512]{1,0:T(8,128)} %get-tuple-element.65.refs_6_) | copy-start | bytes 3145732
  194.5 35.0 %copy-start.5 = (f32[192,512]{1,0:T(8,128)S(1)}, f32[192,512]{1,0:T(8,128)}, u32[]{:S(2)}) copy-start(f32[192,512]{1,0:T(8,128)} %get-tuple-element.83) | copy-start | bytes 1179652
  194.5 35.0 %copy-start.6 = (f32[192,512]{1,0:T(8,128)S(1)}, f32[192,512]{1,0:T(8,128)}, u32[]{:S(2)}) copy-start(f32[192,512]{1,0:T(8,128)} %get-tuple-element.116) | copy-start | bytes 1179652
  221.1 9.2 %copy-start.3 = (f32[512,512]{1,0:T(8,128)S(1)}, f32[512,512]{1,0:T(8,128)}, u32[]{:S(2)}) copy-start(f32[512,512]{1,0:T(8,128)} %get-tuple-element.64.refs_4_) | copy-start | bytes 3145732
  221.2 24.3 %collective-permute-start.37 = (f32[512,512]{1,0:T(8,128)S(1)}, f32[512,512]{1,0:T(8,128)S(1)}, u32[]{:S(2)}, u32[]{:S(2)}) collective-permute-start(f32[512,512]{1,0:T(8,128)S(1)} %orthogonal.3.refs_0_), channel_id=1, source_target_pairs={{0,3},{1,0},{2,1},{8,11},{9,8},{11,10},{16,19},{18,17},{19,18},{25... | collective-permute-start | bytes 3145736 | tf_op jit(solution)/shard_map/ppermute | solution.py:283
  226.2 24.6 %collective-permute-start.38 = (f32[512,512]{1,0:T(8,128)S(1)}, f32[512,512]{1,0:T(8,128)S(1)}, u32[]{:S(2)}, u32[]{:S(2)}) collective-permute-start(f32[512,512]{1,0:T(8,128)S(1)} %orthogonal.3.refs_0_), channel_id=1, source_target_pairs={{0,16},{1,17},{2,18},{8,24},{9,25},{11,27},{16,0},{18,2},{19,3},{2... | collective-permute-start | bytes 3145736 | tf_op jit(solution)/shard_map/ppermute | solution.py:283
  228.1 22.7 %collective-permute-start.39 = (f32[512,512]{1,0:T(8,128)S(1)}, f32[512,512]{1,0:T(8,128)S(1)}, u32[]{:S(2)}, u32[]{:S(2)}) collective-permute-start(f32[512,512]{1,0:T(8,128)S(1)} %orthogonal.3.refs_0_), channel_id=1, source_target_pairs={{0,1},{1,2},{2,3},{8,9},{9,10},{11,8},{16,17},{18,19},{19,16},{25,... | collective-permute-start | bytes 3145736 | tf_op jit(solution)/shard_map/ppermute | solution.py:283
  259.7 27.6 %copy-start = (f32[1,96,4096]{2,1,0:T(8,128)S(1)}, f32[1,96,4096]{2,1,0:T(8,128)}, u32[]{:S(2)}) copy-start(f32[1,96,4096]{2,1,0:T(8,128)} %param.20) | copy-start | bytes 4718596
  259.7 27.6 %copy-start.1 = (f32[4096]{0:T(1024)S(1)}, f32[4096]{0:T(1024)}, u32[]{:S(2)}) copy-start(f32[4096]{0:T(1024)} %param.21) | copy-start | bytes 49156
  (12 other events, 30.9 us)
